TPU v7x, 32 devices: a whole 2x2x4 slice. The times are simulated.
32 devices in a mesh: ctx: 8 (over z, core), exp: 4 (over y, x).
Axes of the slice: x: 2, y: 2, z: 4, core: 2. Of those that a mesh axis runs over, the one named last changes fastest.
Arguments:
- scan_input: bfloat16 [1024, 4096], P('ctx', 'exp'), may hold values from -6 to 6
- step_size: bfloat16 [1024, 4096], P('ctx', 'exp'), may hold values from 0.5 to 2
- decay_rate: float32 [16, 4096], P(None, 'exp'), may hold values from 2e-06 to 0.1
- input_proj: float32 [16, 1024], P(None, 'ctx'), may hold values from -1.5 to 1.5
- output_proj: float32 [16, 1024], P(None, 'ctx'), may hold values from -0.4 to 0.4
- skip_gain: float32 [4096], P('exp'), may hold values from 0.5 to 1.5
- block_states: float32 [8, 16, 4096], P('ctx', None, 'exp'), may hold values from -24 to 24
- end_grad: float32 [16, 4096], P(None, 'exp'), may hold values from -6 to 6
- scan_grad: bfloat16 [1024, 4096], P('ctx', 'exp'), may hold values from -6 to 6
- moe_grad: bfloat16 [1024, 4096], P(('ctx', 'exp')), may hold values from -6 to 6
- route: int32 [1024, 2], P(('ctx', 'exp')), may hold values from 0 to 15, all different within a row; in each aligned block of 32 rows (0 to 31, 32 to 63, ...) at most 8 rows name the same one
- gate_prob: float32 [1024, 2], P(('ctx', 'exp')), may hold values from 0.1 to 0.9
- w_down: bfloat16 [16, 7168, 4096], P('exp', 'ctx'), may hold values from -0.0625 to 0.0625
- hidden_saved: bfloat16 [16, 256, 7168], P('exp', None, 'ctx'), may hold values from -6 to 6
Outputs:
- input_grad: bfloat16 [1024, 4096], P('ctx', 'exp')
- step_grad: bfloat16 [1024, 4096], P('ctx', 'exp')
- in_proj_grad: float32 [16, 1024], P(None, 'ctx')
- out_proj_grad: float32 [16, 1024], P(None, 'ctx')
- decay_grad: float32 [16, 4096], P(None, 'exp')
- down_grad: bfloat16 [16, 7168, 4096], P('exp', 'ctx')
- hidden_grad: bfloat16 [16, 256, 7168], P('exp', None, 'ctx')
Inputs may be any that keep to these rules, and one draw needn't show every extreme that they name: `route`: the experts of one token differ. Within the 32 tokens of one source (aligned blocks of 32 rows) no expert is named more than 8 times, a bound that some block reaches.
All inputs are finite; a program needn't handle non-finite values.
Results may differ from a plain program's by a relative error of at most 0.0049.
Values may be sent and summed in bfloat16 or wider, within the bound.
No kernel may reach another device: no remote copies, remote signals or barrier semaphores. Data moves between devices by JAX's collectives and lax.ppermute only.
A program may use at most 192 MiB of HBM per device.

v0:
```python
import functools
import math

import jax
import jax.numpy as jnp
from jax import lax
from jax.experimental import pallas as pl
from jax.experimental.pallas import tpu as pltpu
from jax.sharding import PartitionSpec as P

EXPERTS = 16
F32 = jnp.float32
BF16 = jnp.bfloat16
LOG2E = math.log2(math.e)
LN2 = math.log(2.0)
LANES = 128
EXTRA = 128
CHUNK = 16
COLUMNS = 512
PIECE = 1024
WIDTHS = (2048, 2048)
SMALL_VMEM = 4 * 1024 * 1024
BOTH = ("ctx", "exp")


def lane_column(matrix, index):
    places = jnp.full(matrix.shape, index, jnp.int32)
    return jnp.take_along_axis(matrix, places, axis=1, mode="promise_in_bounds")


def widen(column, width):
    return jnp.concatenate([column] * (width // LANES), axis=1)


def fold_lanes(value):
    total = value[:, :LANES]
    for start in range(LANES, value.shape[1], LANES):
        total = total + value[:, start : start + LANES]
    return total


def lane_sums(base, partials_s, sums):
    states = sums.shape[0]
    partials = partials_s[...]
    ones = jnp.ones((LANES, sums.shape[1]), BF16)
    high = partials.astype(BF16)
    low = (partials - high.astype(F32)).astype(BF16)
    total = jnp.dot(high, ones, preferred_element_type=F32)
    total += jnp.dot(low, ones, preferred_element_type=F32)
    lane = lax.broadcasted_iota(jnp.int32, sums.shape, 1)
    for k in range(CHUNK):
        sums = jnp.where(lane == base + k, total[k * states : (k + 1) * states, :], sums)
    return sums


def seed_kernel(
    step_ref, inp_ref, grad_ref, rate_ref, cmat_ref, out_ref, step_v, drive_v, inp_v, grad_v
):
    tokens, width = step_ref.shape
    states = rate_ref.shape[0]
    block = pl.ds(pl.multiple_of(pl.program_id(0) * width, width), width)
    steps = step_ref[...].astype(F32)
    inputs = inp_ref[...].astype(F32)
    step_v[:, block] = steps
    drive_v[:, block] = steps * inputs
    inp_v[:, block] = inputs
    grad_v[:, block] = grad_ref[...].astype(F32)
    scaled = rate_ref[...] * -LOG2E
    cmat = cmat_ref[...]
    unroll = CHUNK

    def several(i, running):
        for k in range(unroll):
            t = tokens - 1 - (i * unroll + k)
            ccol = widen(lane_column(cmat, t), width)
            stp = step_v[pl.ds(t, 1), block]
            grad = grad_v[pl.ds(t, 1), block]
            running = jnp.exp2(scaled * stp) * (ccol * grad + running)
        return running

    running = lax.fori_loop(0, tokens // unroll, several, jnp.zeros((states, width), F32))
    out_ref[0:states, :] = running
    out_ref[states : states + 1, :] = jnp.sum(steps, axis=0, keepdims=True)


def fetch_copies(fetch, refs):
    if fetch is None:
        return [], refs
    at, width, outs = fetch
    w_ref, held_v, sems = refs[0], refs[1 + outs], refs[-1]
    refs = [*refs[1 : 1 + outs], *refs[2 + outs : -1]]
    copies = [
        pltpu.make_async_copy(w_ref.at[l, :, pl.ds(at, width)], held_v.at[l], sems.at[l])
        for l in range(held_v.shape[0])
    ]
    return copies, refs


def forward_kernel(
    fetch, step_v, drive_v, grad_v, rate_ref, bmat_ref, first_ref, *refs
):
    copies, refs = fetch_copies(fetch, refs)
    before_v, cols_ref, partials_s = refs
    tokens = step_v.shape[0]
    states, width = rate_ref.shape
    block = pl.ds(pl.multiple_of(pl.program_id(0) * width, width), width)

    @pl.when(pl.program_id(0) == 0)
    def _():
        for copy in copies:
            copy.start()
        cols_ref[...] = jnp.zeros_like(cols_ref)

    scaled = rate_ref[...] * -LOG2E
    bmat = bmat_ref[...]

    def chunk(i, carry):
        state, cols = carry
        base = i * CHUNK
        for k in range(CHUNK):
            t = base + k
            before_v[pl.ds(pl.multiple_of(t * states, states), states), block] = state.astype(BF16)
            bcol = widen(lane_column(bmat, t), width)
            state = (
                jnp.exp2(scaled * step_v[pl.ds(t, 1), block]) * state
                + bcol * drive_v[pl.ds(t, 1), block]
            )
            partials_s[k * states : (k + 1) * states, :] = fold_lanes(
                state * grad_v[pl.ds(t, 1), block]
            )
        return state, lane_sums(base, partials_s, cols)

    _, cols = lax.fori_loop(
        0, tokens // CHUNK, chunk, (first_ref[0], jnp.zeros(cols_ref.shape, F32))
    )
    cols_ref[...] += cols

    @pl.when(pl.program_id(0) == pl.num_programs(0) - 1)
    def _():
        for copy in copies:
            copy.wait()


def adjoint_kernel(
    fetch, step_v, drive_v, inp_v, grad_v, before_v, rate_ref, bmat_ref, cmat_ref, skip_ref,
    end_ref, later_ref, other_ref, out_cols_ref, *refs
):
    copies, refs = fetch_copies(fetch, refs)
    input_ref, stepg_ref, cols_ref, rateg_ref, adj_s, rated_s, partials_s, bdiag_s = refs
    tokens = step_v.shape[0]
    states, width = rate_ref.shape
    block = pl.ds(pl.multiple_of(pl.program_id(0) * width, width), width)
    rate = rate_ref[...]
    scaled = rate * -LOG2E
    cmat = cmat_ref[...]
    skip = skip_ref[...]
    chunks = tokens // CHUNK
    span = CHUNK * states
    ones_diag = jnp.where(
        lax.div(lax.broadcasted_iota(jnp.int32, (CHUNK, span), 1), states)
        == lax.broadcasted_iota(jnp.int32, (CHUNK, span), 0),
        1.0,
        0.0,
    ).astype(BF16)

    @pl.when(pl.program_id(0) == 0)
    def _():
        for copy in copies:
            copy.start()
        cols_ref[0] = jnp.zeros(cols_ref.shape[1:], F32)
        cols_ref[1] = out_cols_ref[...]
        spread_to = jnp.where(
            lax.rem(lax.broadcasted_iota(jnp.int32, (states, span), 1), states)
            == lax.broadcasted_iota(jnp.int32, (states, span), 0),
            1.0,
            0.0,
        ).astype(BF16)
        own = lax.div(lax.broadcasted_iota(jnp.int32, (tokens, span), 1), states) == lax.rem(
            lax.broadcasted_iota(jnp.int32, (tokens, span), 0), CHUNK
        )
        by_token = bmat_ref[...].T
        high = by_token.astype(BF16)
        low = (by_token - high.astype(F32)).astype(BF16)
        for part, value in enumerate((high, low)):
            spread = jnp.dot(value, spread_to, preferred_element_type=F32)
            bdiag_s[part] = jnp.where(own, spread, 0.0).astype(BF16)

    def chunk(i, carry):
        running, rate_acc, cols = carry
        base = (chunks - 1 - i) * CHUNK
        for k in reversed(range(CHUNK)):
            t = base + k
            held = slice(k * states, (k + 1) * states)
            stp = step_v[pl.ds(t, 1), block]
            ccol = widen(lane_column(cmat, t), width)
            adjoint = ccol * grad_v[pl.ds(t, 1), block] + running
            adj_s[held, :] = adjoint.astype(BF16)
            partials_s[held, :] = fold_lanes(adjoint * drive_v[pl.ds(t, 1), block])
            running = jnp.exp2(scaled * stp) * adjoint
            prior = before_v[pl.ds(pl.multiple_of(t * states, states), states), block]
            weighted = running * prior.astype(F32)
            rated_s[held, :] = (scaled * weighted).astype(BF16)
            rate_acc = rate_acc + stp * weighted
        rows = pl.ds(pl.multiple_of(base, CHUNK), CHUNK)
        adjoints = adj_s[...]
        driven = jnp.dot(bdiag_s[0, rows, :], adjoints, preferred_element_type=F32)
        driven += jnp.dot(bdiag_s[1, rows, :], adjoints, preferred_element_type=F32)
        rated = jnp.dot(ones_diag, rated_s[...], preferred_element_type=F32)
        input_ref[rows, :] = (step_v[rows, block] * driven + skip * grad_v[rows, block]).astype(BF16)
        stepg_ref[rows, :] = (inp_v[rows, block] * driven + LN2 * rated).astype(BF16)
        return running, rate_acc, lane_sums(base, partials_s, cols)

    later = later_ref[...]
    beyond = end_ref[...]

    def through(held, value):
        return jnp.exp(-rate * held[states:]) * value + held[:states]

    passed = through(other_ref[...], beyond)
    beyond = jnp.where(ctx_bit(lax.axis_size("ctx") // 2), passed, beyond)
    enter = through(later, beyond)
    _, rate_acc, cols = lax.fori_loop(
        0, chunks, chunk, (enter, jnp.zeros_like(enter), jnp.zeros(cols_ref.shape[1:], F32))
    )
    rateg_ref[...] = -rate_acc
    cols_ref[0] += cols

    @pl.when(pl.program_id(0) == pl.num_programs(0) - 1)
    def _():
        for copy in copies:
            copy.wait()


def ctx_bit(bit):
    return lax.rem(lax.div(lax.axis_index("ctx"), bit), 2) == 0


def fold_kernel(bit, total_ref, later_ref, other_ref, rate_ref, total_out, later_out):
    states = rate_ref.shape[0]
    low = ctx_bit(bit)
    rate = rate_ref[...]
    total, later, other = total_ref[...], later_ref[...], other_ref[...]

    def after(first, second):
        seed = jnp.exp(-rate * first[states:]) * second[:states] + first[:states]
        return seed, first[states:] + second[states:]

    seed, steps = after(jnp.where(low, total, other), jnp.where(low, other, total))
    total_out[:states, :] = seed
    total_out[states:, :] = steps
    seed, steps = after(later, other)
    later_out[:states, :] = jnp.where(low, seed, later[:states])
    later_out[states:, :] = jnp.where(low, steps, later[states:])


def first_fold_kernel(bit, total_ref, other_ref, rate_ref, total_out, later_out):
    states = rate_ref.shape[0]
    low = ctx_bit(bit)
    rate = rate_ref[...]
    total, other = total_ref[...], other_ref[...]
    first, second = jnp.where(low, total, other), jnp.where(low, other, total)
    total_out[:states, :] = jnp.exp(-rate * first[states:]) * second[:states] + first[:states]
    total_out[states:, :] = first[states:] + second[states:]
    later_out[...] = jnp.where(low, other, 0.0)


def exchanged_seeds(seeded, decay_rate):
    count = lax.axis_size("ctx")
    total, later, totals = seeded, None, []
    bit = 1
    while bit < count:
        other = lax.ppermute(total, "ctx", [(i, i ^ bit) for i in range(count)])
        if 2 * bit == count:
            return later, other, totals
        held = [total, other] if later is None else [total, later, other]
        total, later = pl.pallas_call(
            functools.partial(first_fold_kernel if later is None else fold_kernel, bit),
            name=f"fold_{bit}",
            in_specs=[pl.BlockSpec(memory_space=pltpu.VMEM)] * (len(held) + 1),
            out_specs=[pl.BlockSpec(memory_space=pltpu.VMEM)] * 2,
            out_shape=[jax.ShapeDtypeStruct(seeded.shape, F32)] * 2,
            compiler_params=pltpu.CompilerParams(vmem_limit_bytes=SMALL_VMEM),
        )(*held, decay_rate)
        totals.append(total)
        bit *= 2


def scan_call(kernel, name, width, tokens, states, ins, outs, scratch, fetch=None, w_down=None):
    block = min(1024, width)
    whole = pl.BlockSpec(memory_space=pltpu.VMEM)
    kinds = {
        "tok": pl.BlockSpec((tokens, block), lambda j: (0, j)),
        "rate": pl.BlockSpec((states, block), lambda j: (0, j)),
        "seed": pl.BlockSpec((states + 1, block), lambda j: (0, j)),
        "mat": pl.BlockSpec((states, tokens), lambda j: (0, 0)),
        "first": pl.BlockSpec((1, states, block), lambda j: (0, 0, j)),
        "skip": pl.BlockSpec((1, block), lambda j: (0, j)),
        "both": pl.BlockSpec((2, states, tokens), lambda j: (0, 0, 0)),
        "row": whole,
        "state": whole,
    }
    shapes = {
        "tok": jax.ShapeDtypeStruct((tokens, width), BF16),
        "rate": jax.ShapeDtypeStruct((states, width), F32),
        "seed": jax.ShapeDtypeStruct((states + 1, width), F32),
        "mat": jax.ShapeDtypeStruct((states, tokens), F32),
        "both": jax.ShapeDtypeStruct((2, states, tokens), F32),
        "row": pltpu.VMEM((tokens, width), F32),
        "state": pltpu.VMEM((tokens * states, width), BF16),
    }
    scratches = {
        "chunk": pltpu.VMEM((CHUNK * states, block), BF16),
        "sums": pltpu.VMEM((CHUNK * states, LANES), F32),
        "diag": pltpu.VMEM((2, tokens, CHUNK * states), BF16),
    }
    in_specs = [kinds[kind] for kind in ins]
    out_specs = [kinds[kind] for kind in outs]
    out_shape = [shapes[kind] for kind in outs]
    scratch = [scratches[kind] for kind in scratch]
    if fetch is not None:
        local, hidden, _ = w_down.shape
        in_specs.append(pl.BlockSpec(memory_space=pl.ANY))
        out_specs.append(whole)
        out_shape.append(pltpu.VMEM((local, hidden, fetch[1]), BF16))
        scratch.append(pltpu.SemaphoreType.DMA((local,)))
        fetch = (*fetch, len(outs))

    def call(*operands):
        operands = [
            in_vmem(value) if kind in ("row", "state") else value
            for kind, value in zip(ins, operands)
        ]
        if fetch is not None:
            operands.append(w_down)
        return pl.pallas_call(
            kernel if kernel is seed_kernel else functools.partial(kernel, fetch),
            name=name,
            grid=(width // block,),
            in_specs=in_specs,
            out_specs=out_specs,
            out_shape=out_shape,
            scratch_shapes=scratch,
            compiler_params=pltpu.CompilerParams(vmem_limit_bytes=8 * 1024 * 1024),
            cost_estimate=pl.CostEstimate(flops=0, bytes_accessed=0, transcendentals=0),
        )(*operands)

    return call


def in_vmem(value):
    return pltpu.with_memory_space_constraint(value, pltpu.VMEM)


def butterfly_sum(value, axis):
    count = lax.axis_size(axis)
    bit = 1
    while bit < count:
        value = value + lax.ppermute(value, axis, [(i, i ^ bit) for i in range(count)])
        bit *= 2
    return value


def pack_kernel(widths, local, capacity, grad_ref, route_ref, gate_ref, *out_refs):
    tokens = route_ref.shape[1]
    around = lax.axis_size("exp")
    place = lax.rem(lax.axis_index("ctx"), 2) * around + lax.axis_index("exp")
    expert = lax.broadcasted_iota(jnp.int32, (EXPERTS, tokens), 0)
    chosen = [expert == route_ref[j : j + 1, :] for j in range(2)]
    named = jnp.where(chosen[0] | chosen[1], 1.0, 0.0).astype(BF16)
    row = lax.broadcasted_iota(jnp.int32, (tokens, tokens), 0)
    col = lax.broadcasted_iota(jnp.int32, (tokens, tokens), 1)
    earlier = jnp.dot(
        named, jnp.where(row < col, 1.0, 0.0).astype(BF16), preferred_element_type=F32
    )
    spot = lax.broadcasted_iota(jnp.int32, (EXTRA, tokens), 0)
    table = jnp.zeros((EXTRA, tokens), F32)
    for j in range(2):
        rank = jnp.sum(jnp.where(chosen[j], earlier, 0.0), axis=0, keepdims=True)
        number = route_ref[j : j + 1, :]
        owner = lax.div(number, local)
        slot = ((number - owner * local) * (2 * around) + place) * capacity
        prob = gate_ref[j : j + 1, :]
        high = prob.astype(BF16).astype(F32)
        middle = (prob - high).astype(BF16).astype(F32)
        low = prob - high - middle
        fields = (owner.astype(F32), slot.astype(F32) + rank, high, middle, low)
        for k, field in enumerate(fields):
            table = jnp.where(spot == 8 * j + k, field, table)
    extra = lax.dot_general(
        jnp.where(row == col, 1.0, 0.0).astype(BF16),
        table.astype(BF16),
        (((1,), (1,)), ((), ())),
        preferred_element_type=F32,
    )
    start = 0
    for width, out_ref in zip(widths, out_refs):
        out_ref[:, :width] = grad_ref[:, start : start + width]
        start += width
    out_refs[0][:, widths[0] :] = extra.astype(BF16)


def in_hbm(value):
    return pltpu.with_memory_space_constraint(value, pltpu.HBM)


def pack_tokens(moe_grad, route, gate_prob, widths, local, capacity):
    tokens = moe_grad.shape[0]
    vmem = pl.BlockSpec(memory_space=pltpu.VMEM)
    outs = [
        jax.ShapeDtypeStruct((tokens, width + (EXTRA if p == 0 else 0)), BF16)
        for p, width in enumerate(widths)
    ]
    return pl.pallas_call(
        functools.partial(pack_kernel, widths, local, capacity),
        name="pack_tokens",
        in_specs=[vmem] * 3,
        out_specs=[vmem] * len(outs),
        out_shape=outs,
        compiler_params=pltpu.CompilerParams(vmem_limit_bytes=SMALL_VMEM),
    )(in_hbm(moe_grad), in_hbm(route.T), in_hbm(gate_prob.T))


def pairing(partner):
    pairs = []
    for i in range(32):
        z, c, y, x = partner(i // 8, (i // 4) % 2, (i // 2) % 2, i % 2)
        pairs.append((i, ((z * 2 + c) * 2 + y) * 2 + x))
    return pairs


Z_HOPS = [pairing(lambda z, c, y, x, j=j: (z ^ j, c, y, x)) for j in (1, 2, 3)]
CORE_HOP = pairing(lambda z, c, y, x: (z, c ^ 1, y, x))
PLANE_ONE = pairing(lambda z, c, y, x: (z, c, y, x ^ 1) if c == 0 else (z, c, y ^ 1, x))
PLANE_TWO = pairing(lambda z, c, y, x: (z, c, y ^ 1, x) if c == 0 else (z, c, y, x ^ 1))


def after(value, *done):
    return lax.optimization_barrier((value, *done))[0]


def z_hops(value):
    return [lax.ppermute(value, BOTH, hop) for hop in Z_HOPS]


def join_z(own, received):
    return jnp.concatenate([value[None, None] for value in (own, *received)], axis=0)


def join_plane(held, received):
    joined = jnp.concatenate([held, received], axis=1)
    return joined.reshape(-1, joined.shape[-1])


def build_picks(zs, piece_refs, pick_v, gate_v):
    rows = piece_refs[0].shape[0]
    slots = pick_v.shape[1]
    rows_z = rows // zs
    extra = slice(piece_refs[0].shape[1] - EXTRA, piece_refs[0].shape[1])
    me = lax.axis_index("exp").astype(F32)
    for jz in range(zs):
        held = jnp.concatenate(
            [ref[jz * rows_z : (jz + 1) * rows_z, extra] for ref in piece_refs], axis=0
        )
        table = held.astype(F32).T
        row = lax.broadcasted_iota(jnp.int32, (slots, held.shape[0]), 0).astype(F32)
        pick = jnp.zeros(row.shape, F32)
        gate = jnp.zeros(row.shape, F32)
        for j in range(2):
            owner, slot, high, middle, low = [table[8 * j + k : 8 * j + k + 1, :] for k in range(5)]
            hit = jnp.where(owner == me, slot, -1.0) == row
            pick = jnp.where(hit, 1.0, pick)
            gate = jnp.where(hit, (high + middle) + low, gate)
        pick_v[jz] = pick.astype(BF16)
        gate_v[jz] = jnp.broadcast_to(jnp.sum(gate, axis=1, keepdims=True), (slots, LANES))


def expert_kernel(first, last, at, width, own, *refs):
    piece_refs, refs = refs[:4], refs[4:]
    saved_v, w_ref, refs = refs[0], refs[1], refs[2:]
    if not first:
        pick_v, gate_v, sum_v, refs = refs[0], refs[1], refs[2], refs[4:]
    down_ref, hidden_ref, refs = refs[0], refs[1], refs[2:]
    if first:
        pick_v, gate_v, refs = refs[0], refs[1], refs[2:]
    w_copies = []
    if own:
        w_v, w_sems, refs = refs[0], refs[1], refs[2:]
        w_copies = [
            pltpu.make_async_copy(w_ref.at[l, :, pl.ds(at, width)], w_v.at[l], w_sems.at[l])
            for l in range(w_v.shape[0])
        ]
        for copy in w_copies:
            copy.start()
    else:
        w_v = w_ref
    if last:
        hidden_s, hidden_sems, refs = refs[0], refs[1], refs[2:]
    slots_s, stage_s, out_sems = refs
    local, slots, _ = slots_s.shape
    zs = pick_v.shape[0]
    per_z, rows_z = slots // zs, piece_refs[0].shape[0] // zs
    pieces = width // PIECE

    def out_copy(expert, n):
        return pltpu.make_async_copy(
            stage_s.at[n], down_ref.at[expert, :, pl.ds(at + n * PIECE, PIECE)], out_sems.at[n]
        )

    if first:
        build_picks(zs, piece_refs, pick_v, gate_v)
    own_z = lax.div(lax.axis_index("ctx"), 2)
    for jz in range(zs):
        out_rows = pl.ds(pl.multiple_of((own_z ^ jz) * per_z, per_z), per_z)
        for start in range(0, width, COLUMNS):
            span = slice(start, start + COLUMNS)
            held = jnp.concatenate(
                [ref[jz * rows_z : (jz + 1) * rows_z, span] for ref in piece_refs], axis=0
            )
            chosen = jnp.dot(pick_v[jz], held, preferred_element_type=F32)
            value = (chosen * widen(gate_v[jz], COLUMNS)).astype(BF16)
            for expert in range(local):
                slots_s[expert, out_rows, span] = value[expert * per_z : (expert + 1) * per_z, :]

    def one_expert(l, _):
        for n in range(pieces):

            @pl.when(l > 0)
            def _():
                out_copy(l - 1, n).wait()

            for start in range(0, PIECE, COLUMNS):
                span = slice(n * PIECE + start, n * PIECE + start + COLUMNS)
                stage_s[n, :, start : start + COLUMNS] = lax.dot_general(
                    saved_v[l],
                    slots_s[l, :, span],
                    (((0,), (0,)), ((), ())),
                    preferred_element_type=F32,
                ).astype(BF16)
            out_copy(l, n).start()
        if own:
            pltpu.make_async_copy(w_ref.at[l, :, pl.ds(at, width)], w_v.at[l], w_sems.at[l]).wait()
        part = lax.dot_general(
            slots_s[l],
            w_v[l],
            (((1,), (1,)), ((), ())),
            preferred_element_type=F32,
        )
        if not first:
            part = sum_v[l] + part
        if last:
            hidden_s[l] = part.astype(BF16)
            pltpu.make_async_copy(hidden_s.at[l], hidden_ref.at[l], hidden_sems.at[l]).start()
        else:
            hidden_ref[l] = part
        return 0

    lax.fori_loop(0, local, one_expert, 0)
    for n in range(pieces):
        out_copy(local - 1, n).wait()
    if last:
        for l in range(local):
            pltpu.make_async_copy(hidden_s.at[l], hidden_ref.at[l], hidden_sems.at[l]).wait()


def expert_call(part, parts, at, width, pieces, saved, held_w, w_down, carried):
    local, hidden, full = w_down.shape
    slots = saved.shape[1]
    zs = 4
    rows = pieces[0].shape[0]
    first, last = part == 0, part == parts - 1
    whole = pl.BlockSpec(memory_space=pl.ANY)
    kept = pl.BlockSpec(memory_space=pltpu.VMEM)
    own = held_w is None
    operands = [in_vmem(value) for value in (*pieces, saved)]
    operands.append(w_down if own else in_vmem(held_w))
    in_specs = [kept] * 5 + [whole if own else kept]
    aliases = {}
    if not first:
        down, total, pick, gate, *_ = carried
        in_specs += [kept] * 3 + [whole]
        operands += [in_vmem(pick), in_vmem(gate), in_vmem(total), down]
        aliases = {len(operands) - 1: 0}
    out_specs, out_shape = [whole], [jax.ShapeDtypeStruct((local, hidden, full), BF16)]
    scratch = []
    if last:
        out_specs.append(whole)
        out_shape.append(jax.ShapeDtypeStruct((local, slots, hidden), BF16))
        scratch += [pltpu.VMEM((local, slots, hidden), BF16), pltpu.SemaphoreType.DMA((local,))]
    else:
        out_specs.append(kept)
        out_shape.append(pltpu.VMEM((local, slots, hidden), F32))
    if first:
        out_specs += [kept] * 2
        out_shape += [
            pltpu.VMEM((zs, local * slots // zs, 4 * rows // zs), BF16),
            pltpu.VMEM((zs, local * slots // zs, LANES), F32),
        ]
    limit = 12 * 1024 * 1024
    if own:
        scratch = [pltpu.VMEM((local, hidden, width), BF16), pltpu.SemaphoreType.DMA((local,)), *scratch]
        limit += 2 * local * hidden * width
    outs = pl.pallas_call(
        functools.partial(expert_kernel, first, last, at, width, own),
        name=f"experts_{part}",
        in_specs=in_specs,
        out_specs=out_specs,
        out_shape=out_shape,
        scratch_shapes=[
            *scratch,
            pltpu.VMEM((local, slots, width), BF16),
            pltpu.VMEM((width // PIECE, hidden, PIECE), BF16),
            pltpu.SemaphoreType.DMA((width // PIECE,)),
        ],
        input_output_aliases=aliases,
        compiler_params=pltpu.CompilerParams(vmem_limit_bytes=limit),
        cost_estimate=pl.CostEstimate(
            flops=0, bytes_accessed=0, transcendentals=0
        ),
    )(*operands)
    return outs


def slot_buffer(moe_grad, route, gate_prob, capacity):
    pair_count = route.shape[0] * route.shape[1]
    weighted = (gate_prob[:, :, None] * moe_grad.astype(F32)[:, None, :]).astype(BF16)
    weighted = weighted.reshape(pair_count, moe_grad.shape[1])
    flat_route = route.reshape(pair_count)
    onehot = (flat_route[:, None] == jnp.arange(EXPERTS, dtype=jnp.int32)[None, :]).astype(jnp.int32)
    ranks = jnp.sum((jnp.cumsum(onehot, axis=0) - onehot) * onehot, axis=1)
    target = flat_route * capacity + ranks
    placing = (target[:, None] == jnp.arange(EXPERTS * capacity, dtype=jnp.int32)[None, :]).astype(BF16)
    buffer = jnp.einsum("ps,pd->sd", placing, weighted, preferred_element_type=F32).astype(BF16)
    return buffer.reshape(EXPERTS, capacity, moe_grad.shape[1])


def experts_by_slots(moe_grad, route, gate_prob, w_down, hidden_saved, capacity):
    buffer = slot_buffer(moe_grad, route, gate_prob, capacity)
    rows = lax.all_to_all(buffer, "exp", split_axis=0, concat_axis=1, tiled=True)
    rows = lax.all_gather(rows, "ctx", axis=1, tiled=True)
    down = jnp.einsum("lrf,lrd->lfd", hidden_saved, rows, preferred_element_type=F32).astype(BF16)
    hidden = jnp.einsum("lrd,lfd->lrf", rows, w_down, preferred_element_type=F32).astype(BF16)
    return down, hidden


def body(
    scan_input, step_size, decay_rate, input_proj, output_proj, skip_gain, block_states, end_grad,
    scan_grad, moe_grad, route, gate_prob, w_down, hidden_saved,
):
    tokens, width = scan_input.shape
    states = decay_rate.shape[0]
    local, _, full = w_down.shape
    capacity = hidden_saved.shape[1] // (lax.axis_size("ctx") * lax.axis_size("exp"))
    by_tokens = lax.axis_size("ctx") == 8 and lax.axis_size("exp") == 4
    call = functools.partial(scan_call, width=width, tokens=tokens, states=states)
    fetches = (None, None)
    if by_tokens:
        widths = WIDTHS
        fetches = ((0, widths[0]), None)
        assert sum(widths) == full
    seeded, steps, drives, inputs, grads = call(
        seed_kernel, "seed_scan", ins=("tok", "tok", "tok", "rate", "mat"),
        outs=("seed", "row", "row", "row", "row"), scratch=(),
    )(*(in_hbm(value) for value in (step_size, scan_input, scan_grad, decay_rate, output_proj)))
    if by_tokens:
        route = after(route, seeded)
        packed = list(pack_tokens(moe_grad, route, gate_prob, widths, local, capacity))
        from_z = [z_hops(packed[0])]
    later, other, totals = exchanged_seeds(seeded, decay_rate)
    if by_tokens:
        block_states = after(block_states, totals[0], packed[0])
    before, out_cols, *held_w = call(
        forward_kernel, "forward_scan",
        ins=("row", "row", "row", "rate", "mat", "first"),
        outs=("state", "mat"), scratch=("sums",), fetch=fetches[0], w_down=w_down,
    )(steps, drives, grads, decay_rate, input_proj, block_states)
    if by_tokens:
        held_0 = join_z(packed[0], [after(value, out_cols, totals[1]) for value in from_z[0]])
        one_0 = lax.ppermute(held_0, BOTH, PLANE_ONE)
        packed[1] = after(packed[1], held_0)
        from_z.append(z_hops(packed[1]))
        held_0 = join_plane(held_0, after(one_0, other))
        two_0 = lax.ppermute(held_0, BOTH, PLANE_TWO)
        core_0 = lax.ppermute(held_0, BOTH, CORE_HOP)
        later = after(later, held_0)
    input_grad, step_grad, both, rate_local = call(
        adjoint_kernel, "adjoint_scan",
        ins=(
            "row", "row", "row", "row", "state", "rate", "mat", "mat", "skip", "rate", "seed", "seed",
            "mat",
        ),
        outs=("tok", "tok", "both", "rate"),
        scratch=("chunk", "chunk", "sums", "diag"), fetch=fetches[1], w_down=w_down,
    )(
        steps, drives, inputs, grads, before, decay_rate, input_proj, output_proj, skip_gain[None],
        end_grad, later, other, out_cols,
    )
    if by_tokens:
        held_1 = join_z(packed[1], [after(value, both) for value in from_z[1]])
        one_1 = lax.ppermute(held_1, BOTH, PLANE_ONE)
        rate_core = lax.ppermute(rate_local, BOTH, CORE_HOP)
        both_x = lax.ppermute(both, "exp", [(i, i ^ 1) for i in range(4)])
        rate_chip = rate_local + after(rate_core, held_1)
        rate_z1 = lax.ppermute(rate_chip, BOTH, Z_HOPS[0])
        two_0 = after(two_0, rate_chip)
        core_two_0 = lax.ppermute(two_0, BOTH, CORE_HOP)
        held_1 = join_plane(held_1, after(one_1, two_0))
        two_1 = lax.ppermute(held_1, BOTH, PLANE_TWO)
        core_1 = lax.ppermute(held_1, BOTH, CORE_HOP)
        carried = expert_call(
            0, 2, 0, widths[0], [held_0, two_0, core_0, after(core_two_0, held_1)],
            hidden_saved, held_w[0], w_down, None,
        )
        both_pair = both + after(both_x, carried[1])
        both_y = lax.ppermute(both_pair, "exp", [(i, i ^ 2) for i in range(4)])
        rate_pair = rate_chip + after(rate_z1, carried[1])
        rate_z2 = lax.ppermute(rate_pair, BOTH, Z_HOPS[1])
        two_1 = after(two_1, both_pair, rate_pair)
        core_two_1 = lax.ppermute(two_1, BOTH, CORE_HOP)
        both = both_pair + after(both_y, two_1)
        decay_grad = rate_pair + after(rate_z2, two_1)
        down_grad, hidden_grad = expert_call(
            1, 2, widths[0], widths[1], [held_1, two_1, core_1, after(core_two_1, both, decay_grad)],
            hidden_saved, None, w_down, carried,
        )
    else:
        both = butterfly_sum(both, "exp")
        decay_grad = butterfly_sum(rate_local, "ctx")
        down_grad, hidden_grad = experts_by_slots(
            moe_grad, route, gate_prob, w_down, hidden_saved, capacity
        )
    return (input_grad, step_grad, both[0], both[1], decay_grad, down_grad, hidden_grad)


def solution(mesh):
    placed = (
        P("ctx", "exp"),
        P("ctx", "exp"),
        P(None, "exp"),
        P(None, "ctx"),
        P(None, "ctx"),
        P("exp"),
        P("ctx", None, "exp"),
        P(None, "exp"),
        P("ctx", "exp"),
        P(("ctx", "exp"), None),
        P(("ctx", "exp"), None),
        P(("ctx", "exp"), None),
        P("exp", "ctx", None),
        P("exp", None, "ctx"),
    )
    return jax.shard_map(
        body,
        mesh=mesh,
        in_specs=placed,
        out_specs=(
            P("ctx", "exp"),
            P("ctx", "exp"),
            P(None, "ctx"),
            P(None, "ctx"),
            P(None, "exp"),
            P("exp", "ctx", None),
            P("exp", None, "ctx"),
        ),
        check_vma=False,
    )
```

profile of v0, /device:TPU:0, one launch (start us, length us, event | category | flops | bytes accessed | tf_op | source)
XLA Modules:
  0.0 94.7 jit_solution(17996419097095931177)
XLA Ops:
  0.6 0.0 copy-start.1
  0.6 0.0 copy-start.2
  0.7 0.0 copy-start.5
  0.7 3.7 %seed_scan.1 = (f32[17,1024]{1,0:T(8,128)S(1)}, f32[128,1024]{1,0:T(8,128)S(1)}, f32[128,1024]{1,0:T(8,128)S(1)}, f32[128,1024]{1,0:T(8,128)S(1)}, f32[128,1024]{1,0:T(8,128)S(1)}) custom-call(bf16[128,1024]{1,0:T(8,128)(2,1)} %step_ref.1, bf16[128,1024]{1,0:T(8,128)(2,1)} %inp_ref.1, bf16[128,1024]{1,0:T(8,128)(2,1)} %grad_ref.2, f32[16,1024]{1,0:T(8,128)} %rate_ref.9, ...), custom_call_target="tpu_custom_call" | custom-call | tf_op jit(solution)/shard_map/seed_scan/pallas_call | solution.py:335
  4.4 0.5 collective-permute-start
  4.9 1.2 %pack_tokens.1 = (bf16[32,2176]{1,0:T(8,128)(2,1)S(1)}, bf16[32,2048]{1,0:T(8,128)(2,1)S(1)}) custom-call(bf16[32,4096]{1,0:T(8,128)(2,1)} %grad_ref.3, s32[2,32]{1,0:T(2,128)} %bitcast.40, f32[2,32]{1,0:T(2,128)} %bitcast.41), custom_call_target="tpu_custom_call" | custom-call | tf_op jit(solution)/shard_map/pack_tokens/pallas_call | solution.py:413
  6.1 4.6 %collective-permute-start.4 = (bf16[32,2176]{1,0:T(8,128)(2,1)S(1)}, bf16[32,2176]{1,0:T(8,128)(2,1)S(1)}, u32[]{:S(2)}, u32[]{:S(2)}) collective-permute-start(bf16[32,2176]{1,0:T(8,128)(2,1)S(1)} %get-tuple-element.59), channel_id=1, source_target_pairs={{0,24},{1,25},{2,26},{3,27},{4,28},{5,29},{6,30},{7,31},{8,16},{9,... | collective-permute-start | bytes 417800 | tf_op jit(solution)/shard_map/ppermute | solution.py:442
  10.8 0.0 collective-permute-start.3
  10.8 0.6 collective-permute-start.2
  11.4 0.0 collective-permute-done.other_ref
  11.4 0.0 copy-done.1
  11.4 1.5 %collective-permute-start.1 = (f32[17,1024]{1,0:T(8,128)S(1)}, f32[17,1024]{1,0:T(8,128)S(1)}, u32[]{:S(2)}, u32[]{:S(2)}) collective-permute-start(f32[17,1024]{1,0:T(8,128)S(1)} %get-tuple-element.57.total_ref), channel_id=1, source_target_pairs={{0,8},{4,12},{8,0},{12,4},{16,24},{20,28},{24,16},{28,20},{1,9},{5... | collective-permute-start | bytes 208904 | tf_op jit(solution)/shard_map/ppermute | solution.py:272
  12.9 5.3 %forward_scan.1 = (bf16[2048,1024]{1,0:T(8,128)(2,1)S(1)}, f32[16,128]{1,0:T(8,128)S(1)}, bf16[4,896,2048]{2,1,0:T(8,128)(2,1)S(1)}) custom-call(f32[128,1024]{1,0:T(8,128)S(1)} %get-tuple-element.52.step_v, f32[128,1024]{1,0:T(8,128)S(1)} %get-tuple-element.53.drive_v, f32[128,1024]{1,0:T(8,128)S(1)} %get-tuple-element.55.grad_v, f32[16,1024]{1,0:T(8,128)S(1)} %copy-done.1, ...), custom_call_target="tpu_custom_call" | custom-call | tf_op jit(solution)/shard_map/forward_scan/pallas_call | solution.py:335
  18.2 4.3 %collective-permute-done.1.other_ref = f32[17,1024]{1,0:T(8,128)S(1)} collective-permute-done((f32[17,1024]{1,0:T(8,128)S(1)}, f32[17,1024]{1,0:T(8,128)S(1)}, u32[]{:S(2)}, u32[]{:S(2)}) %collective-permute-start.1) | collective-permute-done | bytes 69664 | tf_op jit(solution)/shard_map/ppermute | solution.py:272
  22.5 0.1 fold_2.1
  22.6 0.0 collective-permute-done.4
  22.6 0.7 collective-permute-done.3
  23.3 0.0 collective-permute-done.2
  23.3 0.1 pad_maximum_fusion.2
  23.4 0.0 copy-start.3
  23.4 0.0 copy-start.4
  23.4 0.0 copy-start.6
  23.4 1.6 %collective-permute-start.5 = (bf16[4,1,32,2176]{3,2,1,0:T(8,128)(2,1)S(1)}, bf16[4,1,32,2176]{3,2,1,0:T(8,128)(2,1)S(1)}, u32[]{:S(2)}, u32[]{:S(2)}) collective-permute-start(bf16[4,1,32,2176]{3,2,1,0:T(8,128)(2,1)S(1)} %pad_maximum_fusion.2), channel_id=1, source_target_pairs={{0,1},{1,0},{2,3},{3,2},{4,6},{5,7},{6,4},{7,5},{8,9},{9,8},{10,11... | collective-permute-start | bytes 1671176 | tf_op jit(solution)/shard_map/ppermute | solution.py:678
  24.9 1.7 %collective-permute-start.6 = (f32[17,1024]{1,0:T(8,128)S(1)}, f32[17,1024]{1,0:T(8,128)S(1)}, u32[]{:S(2)}, u32[]{:S(2)}) collective-permute-start(f32[17,1024]{1,0:T(8,128)S(1)} %get-tuple-element.65), channel_id=1, source_target_pairs={{0,16},{4,20},{8,24},{12,28},{16,0},{20,4},{24,8},{28,12},{1,17},{... | collective-permute-start | bytes 208904 | tf_op jit(solution)/shard_map/ppermute | solution.py:272
  26.7 5.7 %collective-permute-done.6.other_ref = f32[17,1024]{1,0:T(8,128)S(1)} collective-permute-done((f32[17,1024]{1,0:T(8,128)S(1)}, f32[17,1024]{1,0:T(8,128)S(1)}, u32[]{:S(2)}, u32[]{:S(2)}) %collective-permute-start.6) | collective-permute-done | bytes 69664 | tf_op jit(solution)/shard_map/ppermute | solution.py:272
  32.4 0.6 collective-permute-done.5
  33.0 0.2 pad_maximum_fusion
  33.1 1.6 %collective-permute-start.8 = (bf16[256,2176]{1,0:T(8,128)(2,1)S(1)}, bf16[256,2176]{1,0:T(8,128)(2,1)S(1)}, u32[]{:S(2)}, u32[]{:S(2)}) collective-permute-start(bf16[256,2176]{1,0:T(8,128)(2,1)S(1)} %bitcast.17), channel_id=1, source_target_pairs={{0,2},{1,3},{2,0},{3,1},{4,5},{5,4},{6,7},{7,6},{8,10},{9,11},{10,... | collective-permute-start | bytes 3342344 | tf_op jit(solution)/shard_map/ppermute | solution.py:682
  34.7 3.6 %collective-permute-start.12 = (bf16[32,2048]{1,0:T(8,128)(2,1)S(1)}, bf16[32,2048]{1,0:T(8,128)(2,1)S(1)}, u32[]{:S(2)}, u32[]{:S(2)}) collective-permute-start(bf16[32,2048]{1,0:T(8,128)(2,1)S(1)} %get-tuple-element.76), channel_id=1, source_target_pairs={{0,24},{1,25},{2,26},{3,27},{4,28},{5,29},{6,30},{7,31},{8,16},{9,... | collective-permute-start | bytes 393224 | tf_op jit(solution)/shard_map/ppermute | solution.py:442
  38.4 0.0 collective-permute-start.11
  38.4 0.7 collective-permute-start.10
  39.1 7.5 %adjoint_scan.1 = (bf16[128,1024]{1,0:T(8,128)(2,1)}, bf16[128,1024]{1,0:T(8,128)(2,1)}, f32[2,16,128]{2,1,0:T(8,128)S(1)}, f32[16,1024]{1,0:T(8,128)S(1)}) custom-call(f32[128,1024]{1,0:T(8,128)S(1)} %get-tuple-element.52.step_v, f32[128,1024]{1,0:T(8,128)S(1)} %get-tuple-element.53.drive_v, f32[128,1024]{1,0:T(8,128)S(1)} %get-tuple-element.54.inp_v, ...), custom_call_target="tpu_custom_call" | custom-call | tf_op jit(solution)/shard_map/adjoint_scan/pallas_call | solution.py:335
  46.6 0.0 collective-permute-done.12
  46.6 1.8 %collective-permute-done.11 = bf16[32,2048]{1,0:T(8,128)(2,1)S(1)} collective-permute-done((bf16[32,2048]{1,0:T(8,128)(2,1)S(1)}, bf16[32,2048]{1,0:T(8,128)(2,1)S(1)}, u32[]{:S(2)}, u32[]{:S(2)}) %collective-permute-start.11) | collective-permute-done | bytes 131104 | tf_op jit(solution)/shard_map/ppermute | solution.py:442
  48.4 0.0 collective-permute-done.10
  48.4 0.1 pad_maximum_fusion.3
  48.5 0.6 collective-permute-start.15
  49.1 0.0 collective-permute-start.9
  49.1 0.5 collective-permute-start.13
  49.6 0.7 collective-permute-done.9
  50.3 0.0 collective-permute-done.8.refs_1_
  50.3 0.2 collective-permute-start.14
  50.6 7.1 %collective-permute-done.15 = bf16[4,1,32,2048]{3,2,1,0:T(8,128)(2,1)S(1)} collective-permute-done((bf16[4,1,32,2048]{3,2,1,0:T(8,128)(2,1)S(1)}, bf16[4,1,32,2048]{3,2,1,0:T(8,128)(2,1)S(1)}, u32[]{:S(2)}, u32[]{:S(2)}) %collective-permute-start.15) | collective-permute-done | bytes 524320 | tf_op jit(solution)/shard_map/ppermute | solution.py:699
  57.7 0.1 pad_maximum_fusion.1
  57.8 1.6 %collective-permute-start.17 = (bf16[256,2048]{1,0:T(8,128)(2,1)S(1)}, bf16[256,2048]{1,0:T(8,128)(2,1)S(1)}, u32[]{:S(2)}, u32[]{:S(2)}) collective-permute-start(bf16[256,2048]{1,0:T(8,128)(2,1)S(1)} %bitcast.20), channel_id=1, source_target_pairs={{0,2},{1,3},{2,0},{3,1},{4,5},{5,4},{6,7},{7,6},{8,10},{9,11},{10,... | collective-permute-start | bytes 3145736 | tf_op jit(solution)/shard_map/ppermute | solution.py:707
  59.4 0.0 collective-permute-start.18
  59.4 0.5 collective-permute-start.7
  59.9 0.0 collective-permute-done.14.refs_3_
  60.0 0.0 collective-permute-done.13.refs_2_
  60.0 11.2 %experts_0.1 = (bf16[4,896,4096]{2,1,0:T(8,128)(2,1)}, f32[4,256,896]{2,1,0:T(8,128)S(1)}, bf16[4,256,256]{2,1,0:T(8,128)(2,1)S(1)}, f32[4,256,128]{2,1,0:T(8,128)S(1)}) custom-call(bf16[256,2176]{1,0:T(8,128)(2,1)S(1)} %bitcast.19, bf16[256,2176]{1,0:T(8,128)(2,1)S(1)} %collective-permute-done.8.refs_1_, ...), custom_call_target="tpu_custom_call" | custom-call | tf_op jit(solution)/shard_map/experts_0/pallas_call | solution.py:602
  71.2 0.0 collective-permute-done.18
  71.2 0.0 collective-permute-done.7
  71.2 1.5 %collective-permute-done.17.refs_1_ = bf16[256,2048]{1,0:T(8,128)(2,1)S(1)} collective-permute-done((bf16[256,2048]{1,0:T(8,128)(2,1)S(1)}, bf16[256,2048]{1,0:T(8,128)(2,1)S(1)}, u32[]{:S(2)}, u32[]{:S(2)}) %collective-permute-start.17) | collective-permute-done | bytes 1048608 | tf_op jit(solution)/shard_map/ppermute | solution.py:707
  72.7 0.0 collective-permute-start.21
  72.7 0.5 collective-permute-start.20
  73.2 1.5 %collective-permute-start.16 = (f32[2,16,128]{2,1,0:T(8,128)S(1)}, f32[2,16,128]{2,1,0:T(8,128)S(1)}, u32[]{:S(2)}, u32[]{:S(2)}) collective-permute-start(f32[2,16,128]{2,1,0:T(8,128)S(1)} %add.16), channel_id=1, source_target_pairs={{0,2},{1,3},{2,0},{3,1},{4,6},{5,7},{6,4},{7,5},{8,10},{9,11},{10,... | collective-permute-start | bytes 49160 | tf_op jit(solution)/shard_map/ppermute | solution.py:714
  74.7 1.0 %collective-permute-start.19 = (f32[16,1024]{1,0:T(8,128)S(1)}, f32[16,1024]{1,0:T(8,128)S(1)}, u32[]{:S(2)}, u32[]{:S(2)}) collective-permute-start(f32[16,1024]{1,0:T(8,128)S(1)} %add.17), channel_id=1, source_target_pairs={{0,16},{1,17},{2,18},{3,19},{4,20},{5,21},{6,22},{7,23},{8,24},{9,... | collective-permute-start | bytes 196616 | tf_op jit(solution)/shard_map/ppermute | solution.py:716
  75.7 1.2 %collective-permute-done.16 = f32[2,16,128]{2,1,0:T(8,128)S(1)} collective-permute-done((f32[2,16,128]{2,1,0:T(8,128)S(1)}, f32[2,16,128]{2,1,0:T(8,128)S(1)}, u32[]{:S(2)}, u32[]{:S(2)}) %collective-permute-start.16) | collective-permute-done | bytes 16416 | tf_op jit(solution)/shard_map/ppermute | solution.py:714
  76.9 0.6 slice_bitcast_fusion
  77.6 2.6 %collective-permute-done.19 = f32[16,1024]{1,0:T(8,128)S(1)} collective-permute-done((f32[16,1024]{1,0:T(8,128)S(1)}, f32[16,1024]{1,0:T(8,128)S(1)}, u32[]{:S(2)}, u32[]{:S(2)}) %collective-permute-start.19) | collective-permute-done | bytes 65568 | tf_op jit(solution)/shard_map/ppermute | solution.py:716
  80.1 0.6 add.19
  80.8 0.0 collective-permute-done.21.refs_3_
  80.8 0.0 collective-permute-done.20.refs_2_
  80.8 14.0 %experts_1.1 = (bf16[4,896,4096]{2,1,0:T(8,128)(2,1)}, bf16[4,256,896]{2,1,0:T(8,128)(2,1)}) custom-call(bf16[256,2048]{1,0:T(8,128)(2,1)S(1)} %bitcast.22, bf16[256,2048]{1,0:T(8,128)(2,1)S(1)} %collective-permute-done.17.refs_1_, bf16[256,2048]{1,0:T(8,128)(2,1)S(1)} %collective-permute-done.20.refs_2_, ...), custom_call_target="tpu_custom_call", output_to_operand_aliasing={{0}: (9, {})} | custom-call | tf_op jit(solution)/shard_map/experts_1/pallas_call | solution.py:602
  (12 shorter events, 0.1 us)
Async XLA Ops:
  0.6 10.7 %copy-start.1 = (f32[16,1024]{1,0:T(8,128)S(1)}, f32[16,1024]{1,0:T(8,128)}, u32[]{:S(2)}) copy-start(f32[16,1024]{1,0:T(8,128)} %rate_ref.9) | copy-start | bytes 196612
  0.6 12.3 %copy-start.2 = (f32[1,16,1024]{2,1,0:T(8,128)S(1)}, f32[1,16,1024]{2,1,0:T(8,128)}, u32[]{:S(2)}) copy-start(f32[1,16,1024]{2,1,0:T(8,128)} %first_ref) | copy-start | bytes 196612
  0.7 12.3 %copy-start.5 = (f32[16,128]{1,0:T(8,128)S(1)}, f32[16,128]{1,0:T(8,128)}, u32[]{:S(2)}) copy-start(f32[16,128]{1,0:T(8,128)} %bmat_ref.3) | copy-start | bytes 24580
  4.4 7.0 %collective-permute-start = (f32[17,1024]{1,0:T(8,128)S(1)}, f32[17,1024]{1,0:T(8,128)S(1)}, u32[]{:S(2)}, u32[]{:S(2)}) collective-permute-start(f32[17,1024]{1,0:T(8,128)S(1)} %get-tuple-element.56.total_ref), channel_id=1, source_target_pairs={{0,4},{4,0},{8,12},{12,8},{16,20},{20,16},{24,28},{28,24},{1,5},{5... | collective-permute-start | bytes 208904 | tf_op jit(solution)/shard_map/ppermute | solution.py:272
  6.1 16.4 %collective-permute-start.4 = (bf16[32,2176]{1,0:T(8,128)(2,1)S(1)}, bf16[32,2176]{1,0:T(8,128)(2,1)S(1)}, u32[]{:S(2)}, u32[]{:S(2)}) collective-permute-start(bf16[32,2176]{1,0:T(8,128)(2,1)S(1)} %get-tuple-element.59), channel_id=1, source_target_pairs={{0,24},{1,25},{2,26},{3,27},{4,28},{5,29},{6,30},{7,31},{8,16},{9,... | collective-permute-start | bytes 417800 | tf_op jit(solution)/shard_map/ppermute | solution.py:442
  10.8 12.5 %collective-permute-start.3 = (bf16[32,2176]{1,0:T(8,128)(2,1)S(1)}, bf16[32,2176]{1,0:T(8,128)(2,1)S(1)}, u32[]{:S(2)}, u32[]{:S(2)}) collective-permute-start(bf16[32,2176]{1,0:T(8,128)(2,1)S(1)} %get-tuple-element.59), channel_id=1, source_target_pairs={{0,16},{1,17},{2,18},{3,19},{4,20},{5,21},{6,22},{7,23},{8,24},{9,... | collective-permute-start | bytes 417800 | tf_op jit(solution)/shard_map/ppermute | solution.py:442
  10.8 12.5 %collective-permute-start.2 = (bf16[32,2176]{1,0:T(8,128)(2,1)S(1)}, bf16[32,2176]{1,0:T(8,128)(2,1)S(1)}, u32[]{:S(2)}, u32[]{:S(2)}) collective-permute-start(bf16[32,2176]{1,0:T(8,128)(2,1)S(1)} %get-tuple-element.59), channel_id=1, source_target_pairs={{0,8},{1,9},{2,10},{3,11},{4,12},{5,13},{6,14},{7,15},{8,0},{9,1},... | collective-permute-start | bytes 417800 | tf_op jit(solution)/shard_map/ppermute | solution.py:442
  11.4 11.1 %collective-permute-start.1 = (f32[17,1024]{1,0:T(8,128)S(1)}, f32[17,1024]{1,0:T(8,128)S(1)}, u32[]{:S(2)}, u32[]{:S(2)}) collective-permute-start(f32[17,1024]{1,0:T(8,128)S(1)} %get-tuple-element.57.total_ref), channel_id=1, source_target_pairs={{0,8},{4,12},{8,0},{12,4},{16,24},{20,28},{24,16},{28,20},{1,9},{5... | collective-permute-start | bytes 208904 | tf_op jit(solution)/shard_map/ppermute | solution.py:272
  23.4 15.8 %copy-start.3 = (f32[16,1024]{1,0:T(8,128)S(1)}, f32[16,1024]{1,0:T(8,128)}, u32[]{:S(2)}) copy-start(f32[16,1024]{1,0:T(8,128)} %end_ref.1) | copy-start | bytes 196612
  23.4 15.8 %copy-start.4 = (f32[16,128]{1,0:T(8,128)S(1)}, f32[16,128]{1,0:T(8,128)}, u32[]{:S(2)}) copy-start(f32[16,128]{1,0:T(8,128)} %cmat_ref.3) | copy-start | bytes 24580
  23.4 15.8 %copy-start.6 = (f32[1024]{0:T(1024)S(1)}, f32[1024]{0:T(1024)}, u32[]{:S(2)}) copy-start(f32[1024]{0:T(1024)} %param.19) | copy-start | bytes 12292
  23.4 9.6 %collective-permute-start.5 = (bf16[4,1,32,2176]{3,2,1,0:T(8,128)(2,1)S(1)}, bf16[4,1,32,2176]{3,2,1,0:T(8,128)(2,1)S(1)}, u32[]{:S(2)}, u32[]{:S(2)}) collective-permute-start(bf16[4,1,32,2176]{3,2,1,0:T(8,128)(2,1)S(1)} %pad_maximum_fusion.2), channel_id=1, source_target_pairs={{0,1},{1,0},{2,3},{3,2},{4,6},{5,7},{6,4},{7,5},{8,9},{9,8},{10,11... | collective-permute-start | bytes 1671176 | tf_op jit(solution)/shard_map/ppermute | solution.py:678
  24.9 7.4 %collective-permute-start.6 = (f32[17,1024]{1,0:T(8,128)S(1)}, f32[17,1024]{1,0:T(8,128)S(1)}, u32[]{:S(2)}, u32[]{:S(2)}) collective-permute-start(f32[17,1024]{1,0:T(8,128)S(1)} %get-tuple-element.65), channel_id=1, source_target_pairs={{0,16},{4,20},{8,24},{12,28},{16,0},{20,4},{24,8},{28,12},{1,17},{... | collective-permute-start | bytes 208904 | tf_op jit(solution)/shard_map/ppermute | solution.py:272
  33.1 17.2 %collective-permute-start.8 = (bf16[256,2176]{1,0:T(8,128)(2,1)S(1)}, bf16[256,2176]{1,0:T(8,128)(2,1)S(1)}, u32[]{:S(2)}, u32[]{:S(2)}) collective-permute-start(bf16[256,2176]{1,0:T(8,128)(2,1)S(1)} %bitcast.17), channel_id=1, source_target_pairs={{0,2},{1,3},{2,0},{3,1},{4,5},{5,4},{6,7},{7,6},{8,10},{9,11},{10,... | collective-permute-start | bytes 3342344 | tf_op jit(solution)/shard_map/ppermute | solution.py:682
  34.7 11.9 %collective-permute-start.12 = (bf16[32,2048]{1,0:T(8,128)(2,1)S(1)}, bf16[32,2048]{1,0:T(8,128)(2,1)S(1)}, u32[]{:S(2)}, u32[]{:S(2)}) collective-permute-start(bf16[32,2048]{1,0:T(8,128)(2,1)S(1)} %get-tuple-element.76), channel_id=1, source_target_pairs={{0,24},{1,25},{2,26},{3,27},{4,28},{5,29},{6,30},{7,31},{8,16},{9,... | collective-permute-start | bytes 393224 | tf_op jit(solution)/shard_map/ppermute | solution.py:442
  38.4 10.0 %collective-permute-start.11 = (bf16[32,2048]{1,0:T(8,128)(2,1)S(1)}, bf16[32,2048]{1,0:T(8,128)(2,1)S(1)}, u32[]{:S(2)}, u32[]{:S(2)}) collective-permute-start(bf16[32,2048]{1,0:T(8,128)(2,1)S(1)} %get-tuple-element.76), channel_id=1, source_target_pairs={{0,16},{1,17},{2,18},{3,19},{4,20},{5,21},{6,22},{7,23},{8,24},{9,... | collective-permute-start | bytes 393224 | tf_op jit(solution)/shard_map/ppermute | solution.py:442
  38.4 10.0 %collective-permute-start.10 = (bf16[32,2048]{1,0:T(8,128)(2,1)S(1)}, bf16[32,2048]{1,0:T(8,128)(2,1)S(1)}, u32[]{:S(2)}, u32[]{:S(2)}) collective-permute-start(bf16[32,2048]{1,0:T(8,128)(2,1)S(1)} %get-tuple-element.76), channel_id=1, source_target_pairs={{0,8},{1,9},{2,10},{3,11},{4,12},{5,13},{6,14},{7,15},{8,0},{9,1},... | collective-permute-start | bytes 393224 | tf_op jit(solution)/shard_map/ppermute | solution.py:442
  48.5 9.2 %collective-permute-start.15 = (bf16[4,1,32,2048]{3,2,1,0:T(8,128)(2,1)S(1)}, bf16[4,1,32,2048]{3,2,1,0:T(8,128)(2,1)S(1)}, u32[]{:S(2)}, u32[]{:S(2)}) collective-permute-start(bf16[4,1,32,2048]{3,2,1,0:T(8,128)(2,1)S(1)} %pad_maximum_fusion.3), channel_id=1, source_target_pairs={{0,1},{1,0},{2,3},{3,2},{4,6},{5,7},{6,4},{7,5},{8,9},{9,8},{10,11... | collective-permute-start | bytes 1572872 | tf_op jit(solution)/shard_map/ppermute | solution.py:699
  49.1 10.9 %copy-start = (bf16[4,256,896]{2,1,0:T(8,128)(2,1)S(1)}, bf16[4,256,896]{2,1,0:T(8,128)(2,1)}, u32[]{:S(2)}) copy-start(bf16[4,256,896]{2,1,0:T(8,128)(2,1)} %refs_4_.3) | copy-start | bytes 5505028
  49.1 1.3 %collective-permute-start.9 = (f32[16,1024]{1,0:T(8,128)S(1)}, f32[16,1024]{1,0:T(8,128)S(1)}, u32[]{:S(2)}, u32[]{:S(2)}) collective-permute-start(f32[16,1024]{1,0:T(8,128)S(1)} %get-tuple-element.74), channel_id=1, source_target_pairs={{0,4},{1,5},{2,6},{3,7},{4,0},{5,1},{6,2},{7,3},{8,12},{9,13},{10,... | collective-permute-start | bytes 196616 | tf_op jit(solution)/shard_map/ppermute | solution.py:700
  49.1 10.9 %collective-permute-start.13 = (bf16[256,2176]{1,0:T(8,128)(2,1)S(1)}, bf16[256,2176]{1,0:T(8,128)(2,1)S(1)}, u32[]{:S(2)}, u32[]{:S(2)}) collective-permute-start(bf16[256,2176]{1,0:T(8,128)(2,1)S(1)} %bitcast.18), channel_id=1, source_target_pairs={{0,4},{1,5},{2,6},{3,7},{4,0},{5,1},{6,2},{7,3},{8,12},{9,13},{10,... | collective-permute-start | bytes 3342344 | tf_op jit(solution)/shard_map/ppermute | solution.py:683
  50.3 9.6 %collective-permute-start.14 = (bf16[256,2176]{1,0:T(8,128)(2,1)S(1)}, bf16[256,2176]{1,0:T(8,128)(2,1)S(1)}, u32[]{:S(2)}, u32[]{:S(2)}) collective-permute-start(bf16[256,2176]{1,0:T(8,128)(2,1)S(1)} %collective-permute-done.8.refs_1_), channel_id=1, source_target_pairs={{0,4},{1,5},{2,6},{3,7},{4,0},{5,1},{6,2},{7,3},{8,12},{9,13},{10,... | collective-permute-start | bytes 3342344 | tf_op jit(solution)/shard_map/ppermute | solution.py:705
  57.8 14.9 %collective-permute-start.17 = (bf16[256,2048]{1,0:T(8,128)(2,1)S(1)}, bf16[256,2048]{1,0:T(8,128)(2,1)S(1)}, u32[]{:S(2)}, u32[]{:S(2)}) collective-permute-start(bf16[256,2048]{1,0:T(8,128)(2,1)S(1)} %bitcast.20), channel_id=1, source_target_pairs={{0,2},{1,3},{2,0},{3,1},{4,5},{5,4},{6,7},{7,6},{8,10},{9,11},{10,... | collective-permute-start | bytes 3145736 | tf_op jit(solution)/shard_map/ppermute | solution.py:707
  59.4 11.8 %collective-permute-start.18 = (f32[16,1024]{1,0:T(8,128)S(1)}, f32[16,1024]{1,0:T(8,128)S(1)}, u32[]{:S(2)}, u32[]{:S(2)}) collective-permute-start(f32[16,1024]{1,0:T(8,128)S(1)} %add.15), channel_id=1, source_target_pairs={{0,8},{1,9},{2,10},{3,11},{4,12},{5,13},{6,14},{7,15},{8,0},{9,1},... | collective-permute-start | bytes 196616 | tf_op jit(solution)/shard_map/ppermute | solution.py:703
  59.4 11.8 %collective-permute-start.7 = (f32[2,16,128]{2,1,0:T(8,128)S(1)}, f32[2,16,128]{2,1,0:T(8,128)S(1)}, u32[]{:S(2)}, u32[]{:S(2)}) collective-permute-start(f32[2,16,128]{2,1,0:T(8,128)S(1)} %get-tuple-element.73), channel_id=1, source_target_pairs={{0,1},{1,0},{2,3},{3,2},{4,5},{5,4},{6,7},{7,6},{8,9},{9,8},{10,11... | collective-permute-start | bytes 49160 | tf_op jit(solution)/shard_map/ppermute | solution.py:701
  72.7 8.1 %collective-permute-start.21 = (bf16[256,2048]{1,0:T(8,128)(2,1)S(1)}, bf16[256,2048]{1,0:T(8,128)(2,1)S(1)}, u32[]{:S(2)}, u32[]{:S(2)}) collective-permute-start(bf16[256,2048]{1,0:T(8,128)(2,1)S(1)} %collective-permute-done.17.refs_1_), channel_id=1, source_target_pairs={{0,4},{1,5},{2,6},{3,7},{4,0},{5,1},{6,2},{7,3},{8,12},{9,13},{10,... | collective-permute-start | bytes 3145736 | tf_op jit(solution)/shard_map/ppermute | solution.py:718
  72.7 8.1 %collective-permute-start.20 = (bf16[256,2048]{1,0:T(8,128)(2,1)S(1)}, bf16[256,2048]{1,0:T(8,128)(2,1)S(1)}, u32[]{:S(2)}, u32[]{:S(2)}) collective-permute-start(bf16[256,2048]{1,0:T(8,128)(2,1)S(1)} %bitcast.21), channel_id=1, source_target_pairs={{0,4},{1,5},{2,6},{3,7},{4,0},{5,1},{6,2},{7,3},{8,12},{9,13},{10,... | collective-permute-start | bytes 3145736 | tf_op jit(solution)/shard_map/ppermute | solution.py:708
  73.2 3.7 %collective-permute-start.16 = (f32[2,16,128]{2,1,0:T(8,128)S(1)}, f32[2,16,128]{2,1,0:T(8,128)S(1)}, u32[]{:S(2)}, u32[]{:S(2)}) collective-permute-start(f32[2,16,128]{2,1,0:T(8,128)S(1)} %add.16), channel_id=1, source_target_pairs={{0,2},{1,3},{2,0},{3,1},{4,6},{5,7},{6,4},{7,5},{8,10},{9,11},{10,... | collective-permute-start | bytes 49160 | tf_op jit(solution)/shard_map/ppermute | solution.py:714
  74.7 5.4 %collective-permute-start.19 = (f32[16,1024]{1,0:T(8,128)S(1)}, f32[16,1024]{1,0:T(8,128)S(1)}, u32[]{:S(2)}, u32[]{:S(2)}) collective-permute-start(f32[16,1024]{1,0:T(8,128)S(1)} %add.17), channel_id=1, source_target_pairs={{0,16},{1,17},{2,18},{3,19},{4,20},{5,21},{6,22},{7,23},{8,24},{9,... | collective-permute-start | bytes 196616 | tf_op jit(solution)/shard_map/ppermute | solution.py:716
where the time goes:
time: 94.9 us; the launch traced here: 94.7 us
  Pallas kernels  43 us (45%)
  waiting for transfers between devices  26.2 us (28%)
  starting transfers between devices  23 us (24%)
  other arithmetic  1.1 us (1%)
    pallas_call x2, Pallas kernels, expert_call(): pl.pallas_call(functools.partial(expert_kernel, first, last, at, width, o...  25.2 us
    pallas_call x3, Pallas kernels, call(): pl.pallas_call(kernel if kernel is seed_kernel else functools.partial(ker...  16.5 us
    ppermute x3, waiting for transfers between devices, exchanged_seeds(): other = lax.ppermute(total, 'ctx', [(i, i ^ bit) for i in range(count)])  10 us
    ppermute x6, starting transfers between devices, z_hops(): return [lax.ppermute(value, BOTH, hop) for hop in Z_HOPS]  9.6 us
    ppermute x1, waiting for transfers between devices, body(): one_1 = lax.ppermute(held_1, BOTH, PLANE_ONE)  7.14 us
    ppermute x3, starting transfers between devices, exchanged_seeds(): other = lax.ppermute(total, 'ctx', [(i, i ^ bit) for i in range(count)])  3.73 us
    ppermute x1, waiting for transfers between devices, body(): rate_z2 = lax.ppermute(rate_pair, BOTH, Z_HOPS[1])  2.57 us
    ppermute x6, waiting for transfers between devices, z_hops(): return [lax.ppermute(value, BOTH, hop) for hop in Z_HOPS]  2.44 us
  transfers between devices with their start and end apart: 22, of which 10 were waited for; matrix products, arithmetic and copies ran while one was open for 2% of the time, Pallas kernels for 27%

commit v1 on v0

--- a/solution.py
+++ b/solution.py
@@ -18,6 +18,9 @@
 CHUNK = 16
 COLUMNS = 512
 PIECE = 1024
+MICRO = 1_150_000_000
+EXPERT_COST = 0
+ADJOINT = 12
 WIDTHS = (2048, 2048)
 SMALL_VMEM = 4 * 1024 * 1024
 BOTH = ("ctx", "exp")
@@ -86,7 +89,7 @@
 def fetch_copies(fetch, refs):
     if fetch is None:
         return [], refs
-    at, width, outs = fetch
+    at, width, _, outs = fetch
     w_ref, held_v, sems = refs[0], refs[1 + outs], refs[-1]
     refs = [*refs[1 : 1 + outs], *refs[2 + outs : -1]]
     copies = [
@@ -210,15 +213,15 @@
         stepg_ref[rows, :] = (inp_v[rows, block] * driven + LN2 * rated).astype(BF16)
         return running, rate_acc, lane_sums(base, partials_s, cols)
 
-    later = later_ref[...]
     beyond = end_ref[...]
 
-    def through(held, value):
-        return jnp.exp(-rate * held[states:]) * value + held[:states]
-
-    passed = through(other_ref[...], beyond)
+    def through(ref, value):
+        seed, steps = read_map(ref, states)
+        return jnp.exp(-rate * steps) * value + seed
+
+    passed = through(other_ref, beyond)
     beyond = jnp.where(ctx_bit(lax.axis_size("ctx") // 2), passed, beyond)
-    enter = through(later, beyond)
+    enter = through(later_ref, beyond)
     _, rate_acc, cols = lax.fori_loop(
         0, chunks, chunk, (enter, jnp.zeros_like(enter), jnp.zeros(cols_ref.shape[1:], F32))
     )
@@ -235,63 +238,79 @@
     return lax.rem(lax.div(lax.axis_index("ctx"), bit), 2) == 0
 
 
-def fold_kernel(bit, total_ref, later_ref, other_ref, rate_ref, total_out, later_out):
+def read_map(ref, states):
+    held = ref[...].astype(F32)
+    steps = held[states : states + 1]
+    if ref.dtype == BF16:
+        steps = steps + held[states + 1 : states + 2]
+    return held[:states], steps
+
+
+def write_map(seed, steps, out_ref, sent_ref):
+    states = seed.shape[0]
+    out_ref[:states, :] = seed
+    out_ref[states:, :] = steps
+    if sent_ref is not None:
+        high = steps.astype(BF16).astype(F32)
+        sent_ref[...] = jnp.concatenate([seed, high, steps - high], axis=0).astype(BF16)
+
+
+def fold_kernel(bit, total_ref, later_ref, other_ref, rate_ref, total_out, later_out, sent_out):
     states = rate_ref.shape[0]
     low = ctx_bit(bit)
     rate = rate_ref[...]
-    total, later, other = total_ref[...], later_ref[...], other_ref[...]
+    total, other = read_map(total_ref, states), read_map(other_ref, states)
 
     def after(first, second):
-        seed = jnp.exp(-rate * first[states:]) * second[:states] + first[:states]
-        return seed, first[states:] + second[states:]
-
-    seed, steps = after(jnp.where(low, total, other), jnp.where(low, other, total))
-    total_out[:states, :] = seed
-    total_out[states:, :] = steps
-    seed, steps = after(later, other)
-    later_out[:states, :] = jnp.where(low, seed, later[:states])
-    later_out[states:, :] = jnp.where(low, steps, later[states:])
-
-
-def first_fold_kernel(bit, total_ref, other_ref, rate_ref, total_out, later_out):
-    states = rate_ref.shape[0]
-    low = ctx_bit(bit)
-    rate = rate_ref[...]
-    total, other = total_ref[...], other_ref[...]
-    first, second = jnp.where(low, total, other), jnp.where(low, other, total)
-    total_out[:states, :] = jnp.exp(-rate * first[states:]) * second[:states] + first[:states]
-    total_out[states:, :] = first[states:] + second[states:]
-    later_out[...] = jnp.where(low, other, 0.0)
+        return jnp.exp(-rate * first[1]) * second[0] + first[0], first[1] + second[1]
+
+    def chosen(one, two):
+        return jnp.where(low, one[0], two[0]), jnp.where(low, one[1], two[1])
+
+    write_map(*after(chosen(total, other), chosen(other, total)), total_out, sent_out)
+    if later_ref is None:
+        later_out[:states, :] = jnp.where(low, other[0], 0.0)
+        later_out[states:, :] = jnp.where(low, other[1], 0.0)
+    else:
+        later = read_map(later_ref, states)
+        write_map(*chosen(after(later, other), later), later_out, None)
+
+
+def first_fold_kernel(bit, total_ref, other_ref, rate_ref, total_out, later_out, sent_out):
+    fold_kernel(bit, total_ref, None, other_ref, rate_ref, total_out, later_out, sent_out)
 
 
 def exchanged_seeds(seeded, decay_rate):
     count = lax.axis_size("ctx")
-    total, later, totals = seeded, None, []
+    states, width = decay_rate.shape
+    total, later, totals, sent = seeded, None, [], seeded
     bit = 1
     while bit < count:
-        other = lax.ppermute(total, "ctx", [(i, i ^ bit) for i in range(count)])
+        other = lax.ppermute(sent, "ctx", [(i, i ^ bit) for i in range(count)])
         if 2 * bit == count:
             return later, other, totals
         held = [total, other] if later is None else [total, later, other]
-        total, later = pl.pallas_call(
+        total, later, sent = pl.pallas_call(
             functools.partial(first_fold_kernel if later is None else fold_kernel, bit),
             name=f"fold_{bit}",
             in_specs=[pl.BlockSpec(memory_space=pltpu.VMEM)] * (len(held) + 1),
-            out_specs=[pl.BlockSpec(memory_space=pltpu.VMEM)] * 2,
-            out_shape=[jax.ShapeDtypeStruct(seeded.shape, F32)] * 2,
+            out_specs=[pl.BlockSpec(memory_space=pltpu.VMEM)] * 3,
+            out_shape=[jax.ShapeDtypeStruct(seeded.shape, F32)] * 2
+            + [jax.ShapeDtypeStruct((states + 2, width), BF16)],
             compiler_params=pltpu.CompilerParams(vmem_limit_bytes=SMALL_VMEM),
-        )(*held, decay_rate)
+        )(*held, in_hbm(decay_rate))
         totals.append(total)
         bit *= 2
 
 
-def scan_call(kernel, name, width, tokens, states, ins, outs, scratch, fetch=None, w_down=None):
+def scan_call(kernel, name, width, tokens, states, ins, outs, scratch, fetch=None, w_down=None, micros=0):
     block = min(1024, width)
     whole = pl.BlockSpec(memory_space=pltpu.VMEM)
     kinds = {
         "tok": pl.BlockSpec((tokens, block), lambda j: (0, j)),
         "rate": pl.BlockSpec((states, block), lambda j: (0, j)),
         "seed": pl.BlockSpec((states + 1, block), lambda j: (0, j)),
+        "sent": pl.BlockSpec((states + 2, block), lambda j: (0, j)),
         "mat": pl.BlockSpec((states, tokens), lambda j: (0, 0)),
         "first": pl.BlockSpec((1, states, block), lambda j: (0, 0, j)),
         "skip": pl.BlockSpec((1, block), lambda j: (0, j)),
@@ -318,11 +337,11 @@
     out_shape = [shapes[kind] for kind in outs]
     scratch = [scratches[kind] for kind in scratch]
     if fetch is not None:
-        local, hidden, _ = w_down.shape
+        hidden = w_down.shape[1]
         in_specs.append(pl.BlockSpec(memory_space=pl.ANY))
         out_specs.append(whole)
-        out_shape.append(pltpu.VMEM((local, hidden, fetch[1]), BF16))
-        scratch.append(pltpu.SemaphoreType.DMA((local,)))
+        out_shape.append(pltpu.VMEM((fetch[2], hidden, fetch[1]), BF16))
+        scratch.append(pltpu.SemaphoreType.DMA((fetch[2],)))
         fetch = (*fetch, len(outs))
 
     def call(*operands):
@@ -331,7 +350,7 @@
             for kind, value in zip(ins, operands)
         ]
         if fetch is not None:
-            operands.append(w_down)
+            operands.append(in_hbm(w_down))
         return pl.pallas_call(
             kernel if kernel is seed_kernel else functools.partial(kernel, fetch),
             name=name,
@@ -341,7 +360,9 @@
             out_shape=out_shape,
             scratch_shapes=scratch,
             compiler_params=pltpu.CompilerParams(vmem_limit_bytes=8 * 1024 * 1024),
-            cost_estimate=pl.CostEstimate(flops=0, bytes_accessed=0, transcendentals=0),
+            cost_estimate=pl.CostEstimate(
+                flops=MICRO * micros, bytes_accessed=0, transcendentals=0
+            ),
         )(*operands)
 
     return call
@@ -442,13 +463,75 @@
     return [lax.ppermute(value, BOTH, hop) for hop in Z_HOPS]
 
 
+def small_call(kernel, name, shape, *operands, dtype=BF16, limit=2 * 1024 * 1024):
+    kept = pl.BlockSpec(memory_space=pltpu.VMEM)
+    return pl.pallas_call(
+        kernel,
+        name=name,
+        in_specs=[kept] * len(operands),
+        out_specs=kept,
+        out_shape=pltpu.VMEM(shape, dtype),
+        compiler_params=pltpu.CompilerParams(vmem_limit_bytes=limit),
+        cost_estimate=pl.CostEstimate(flops=0, bytes_accessed=0, transcendentals=0),
+    )(*(in_vmem(value) for value in operands))
+
+
+def add_kernel(one_ref, two_ref, out_ref):
+    out_ref[...] = (one_ref[...] + two_ref[...]).astype(out_ref.dtype)
+
+
+def added(one, two, dtype=F32):
+    return small_call(add_kernel, "add_two", one.shape, one, two, dtype=dtype)
+
+
+def add_four_kernel(a_ref, b_ref, c_ref, d_ref, out_ref):
+    a, b, c, d = (ref[...].astype(F32) for ref in (a_ref, b_ref, c_ref, d_ref))
+    out_ref[...] = (a + b) + (c + d)
+
+
+def added_four(*values):
+    return small_call(add_four_kernel, "add_four", values[0].shape, *values, dtype=F32)
+
+
+def split_add_kernel(one_ref, two_ref, first_ref, second_ref):
+    first_ref[...] = one_ref[0] + two_ref[0]
+    second_ref[...] = one_ref[1] + two_ref[1]
+
+
+def split_added(one, two):
+    kept = pl.BlockSpec(memory_space=pltpu.VMEM)
+    return pl.pallas_call(
+        split_add_kernel,
+        name="split_add",
+        in_specs=[kept] * 2,
+        out_specs=[kept] * 2,
+        out_shape=[jax.ShapeDtypeStruct(one.shape[1:], one.dtype)] * 2,
+        compiler_params=pltpu.CompilerParams(vmem_limit_bytes=2 * 1024 * 1024),
+        cost_estimate=pl.CostEstimate(flops=0, bytes_accessed=0, transcendentals=0),
+    )(in_vmem(one), in_vmem(two))
+
+
+def join_z_kernel(*refs):
+    for z, ref in enumerate(refs[:-1]):
+        refs[-1][z] = ref[...]
+
+
 def join_z(own, received):
-    return jnp.concatenate([value[None, None] for value in (own, *received)], axis=0)
+    shape = (1 + len(received), *own.shape)
+    return small_call(join_z_kernel, "join_z", shape, own, *received)
+
+
+def join_plane_kernel(held_ref, received_ref, out_ref):
+    zs, tokens, _ = held_ref.shape
+    for z in range(zs):
+        at = 2 * tokens * z
+        out_ref[at : at + tokens, :] = held_ref[z]
+        out_ref[at + tokens : at + 2 * tokens, :] = received_ref[z]
 
 
 def join_plane(held, received):
-    joined = jnp.concatenate([held, received], axis=1)
-    return joined.reshape(-1, joined.shape[-1])
+    zs, tokens, width = held.shape
+    return small_call(join_plane_kernel, "join_plane", (2 * zs * tokens, width), held, received)
 
 
 def build_picks(zs, piece_refs, pick_v, gate_v):
@@ -476,23 +559,25 @@
 
 def expert_kernel(first, last, at, width, own, *refs):
     piece_refs, refs = refs[:4], refs[4:]
-    saved_v, w_ref, refs = refs[0], refs[1], refs[2:]
+    saved_v, held_v, refs = refs[0], refs[1], refs[2:]
+    ready = held_v.shape[0]
+    if own:
+        w_ref, refs = refs[0], refs[1:]
     if not first:
         pick_v, gate_v, sum_v, refs = refs[0], refs[1], refs[2], refs[4:]
     down_ref, hidden_ref, refs = refs[0], refs[1], refs[2:]
     if first:
         pick_v, gate_v, refs = refs[0], refs[1], refs[2:]
-    w_copies = []
     if own:
         w_v, w_sems, refs = refs[0], refs[1], refs[2:]
-        w_copies = [
-            pltpu.make_async_copy(w_ref.at[l, :, pl.ds(at, width)], w_v.at[l], w_sems.at[l])
-            for l in range(w_v.shape[0])
-        ]
-        for copy in w_copies:
-            copy.start()
-    else:
-        w_v = w_ref
+
+        def w_copy(l):
+            return pltpu.make_async_copy(
+                w_ref.at[ready + l, :, pl.ds(at, width)], w_v.at[l], w_sems.at[l]
+            )
+
+        for l in range(w_v.shape[0]):
+            w_copy(l).start()
     if last:
         hidden_s, hidden_sems, refs = refs[0], refs[1], refs[2:]
     slots_s, stage_s, out_sems = refs
@@ -521,7 +606,7 @@
             for expert in range(local):
                 slots_s[expert, out_rows, span] = value[expert * per_z : (expert + 1) * per_z, :]
 
-    def one_expert(l, _):
+    def one_expert(fetched, l, _):
         for n in range(pieces):
 
             @pl.when(l > 0)
@@ -537,11 +622,11 @@
                     preferred_element_type=F32,
                 ).astype(BF16)
             out_copy(l, n).start()
-        if own:
-            pltpu.make_async_copy(w_ref.at[l, :, pl.ds(at, width)], w_v.at[l], w_sems.at[l]).wait()
+        if fetched:
+            w_copy(l - ready).wait()
         part = lax.dot_general(
             slots_s[l],
-            w_v[l],
+            w_v[l - ready] if fetched else held_v[l],
             (((1,), (1,)), ((), ())),
             preferred_element_type=F32,
         )
@@ -554,7 +639,9 @@
             hidden_ref[l] = part
         return 0
 
-    lax.fori_loop(0, local, one_expert, 0)
+    lax.fori_loop(0, ready, functools.partial(one_expert, False), 0)
+    if own:
+        lax.fori_loop(ready, local, functools.partial(one_expert, True), 0)
     for n in range(pieces):
         out_copy(local - 1, n).wait()
     if last:
@@ -570,10 +657,12 @@
     first, last = part == 0, part == parts - 1
     whole = pl.BlockSpec(memory_space=pl.ANY)
     kept = pl.BlockSpec(memory_space=pltpu.VMEM)
-    own = held_w is None
-    operands = [in_vmem(value) for value in (*pieces, saved)]
-    operands.append(w_down if own else in_vmem(held_w))
-    in_specs = [kept] * 5 + [whole if own else kept]
+    own = local - held_w.shape[0]
+    operands = [in_vmem(value) for value in (*pieces, saved, held_w)]
+    in_specs = [kept] * 6
+    if own:
+        operands.append(in_hbm(w_down))
+        in_specs.append(whole)
     aliases = {}
     if not first:
         down, total, pick, gate, *_ = carried
@@ -597,8 +686,8 @@
         ]
     limit = 12 * 1024 * 1024
     if own:
-        scratch = [pltpu.VMEM((local, hidden, width), BF16), pltpu.SemaphoreType.DMA((local,)), *scratch]
-        limit += 2 * local * hidden * width
+        scratch = [pltpu.VMEM((own, hidden, width), BF16), pltpu.SemaphoreType.DMA((own,)), *scratch]
+        limit += 2 * own * hidden * width
     outs = pl.pallas_call(
         functools.partial(expert_kernel, first, last, at, width, own),
         name=f"experts_{part}",
@@ -614,7 +703,7 @@
         input_output_aliases=aliases,
         compiler_params=pltpu.CompilerParams(vmem_limit_bytes=limit),
         cost_estimate=pl.CostEstimate(
-            flops=0, bytes_accessed=0, transcendentals=0
+            flops=EXPERT_COST if first else 0, bytes_accessed=0, transcendentals=0
         ),
     )(*operands)
     return outs
@@ -655,7 +744,7 @@
     fetches = (None, None)
     if by_tokens:
         widths = WIDTHS
-        fetches = ((0, widths[0]), None)
+        fetches = ((0, widths[0], local), (widths[0], widths[1], local - 1))
         assert sum(widths) == full
     seeded, steps, drives, inputs, grads = call(
         seed_kernel, "seed_scan", ins=("tok", "tok", "tok", "rate", "mat"),
@@ -672,7 +761,7 @@
         forward_kernel, "forward_scan",
         ins=("row", "row", "row", "rate", "mat", "first"),
         outs=("state", "mat"), scratch=("sums",), fetch=fetches[0], w_down=w_down,
-    )(steps, drives, grads, decay_rate, input_proj, block_states)
+    )(steps, drives, grads, in_hbm(decay_rate), in_hbm(input_proj), in_hbm(block_states))
     if by_tokens:
         held_0 = join_z(packed[0], [after(value, out_cols, totals[1]) for value in from_z[0]])
         one_0 = lax.ppermute(held_0, BOTH, PLANE_ONE)
@@ -682,26 +771,29 @@
         two_0 = lax.ppermute(held_0, BOTH, PLANE_TWO)
         core_0 = lax.ppermute(held_0, BOTH, CORE_HOP)
         later = after(later, held_0)
-    input_grad, step_grad, both, rate_local = call(
+    input_grad, step_grad, both, rate_local, *more_w = call(
         adjoint_kernel, "adjoint_scan",
         ins=(
-            "row", "row", "row", "row", "state", "rate", "mat", "mat", "skip", "rate", "seed", "seed",
+            "row", "row", "row", "row", "state", "rate", "mat", "mat", "skip", "rate", "seed", "sent",
             "mat",
         ),
         outs=("tok", "tok", "both", "rate"),
-        scratch=("chunk", "chunk", "sums", "diag"), fetch=fetches[1], w_down=w_down,
+        scratch=("chunk", "chunk", "sums", "diag"), fetch=fetches[1], w_down=w_down, micros=ADJOINT,
     )(
-        steps, drives, inputs, grads, before, decay_rate, input_proj, output_proj, skip_gain[None],
-        end_grad, later, other, out_cols,
+        steps, drives, inputs, grads, before, in_hbm(decay_rate), in_hbm(input_proj),
+        in_hbm(output_proj), in_hbm(skip_gain[None]), in_hbm(end_grad), later, other, out_cols,
     )
     if by_tokens:
-        held_1 = join_z(packed[1], [after(value, both) for value in from_z[1]])
-        one_1 = lax.ppermute(held_1, BOTH, PLANE_ONE)
         rate_core = lax.ppermute(rate_local, BOTH, CORE_HOP)
         both_x = lax.ppermute(both, "exp", [(i, i ^ 1) for i in range(4)])
-        rate_chip = rate_local + after(rate_core, held_1)
-        rate_z1 = lax.ppermute(rate_chip, BOTH, Z_HOPS[0])
-        two_0 = after(two_0, rate_chip)
+        rate_chip = added(rate_local, rate_core, BF16)
+        both_pair = added(both, after(both_x, rate_chip))
+        both_y = lax.ppermute(both_pair, "exp", [(i, i ^ 2) for i in range(4)])
+        held_1 = join_z(packed[1], [after(value, both_pair) for value in from_z[1]])
+        one_1 = lax.ppermute(held_1, BOTH, PLANE_ONE)
+        rate_z = z_hops(after(rate_chip, held_1))
+        decay_grad = added_four(rate_chip, *rate_z)
+        two_0 = after(two_0, decay_grad)
         core_two_0 = lax.ppermute(two_0, BOTH, CORE_HOP)
         held_1 = join_plane(held_1, after(one_1, two_0))
         two_1 = lax.ppermute(held_1, BOTH, PLANE_TWO)
@@ -710,17 +802,12 @@
             0, 2, 0, widths[0], [held_0, two_0, core_0, after(core_two_0, held_1)],
             hidden_saved, held_w[0], w_down, None,
         )
-        both_pair = both + after(both_x, carried[1])
-        both_y = lax.ppermute(both_pair, "exp", [(i, i ^ 2) for i in range(4)])
-        rate_pair = rate_chip + after(rate_z1, carried[1])
-        rate_z2 = lax.ppermute(rate_pair, BOTH, Z_HOPS[1])
-        two_1 = after(two_1, both_pair, rate_pair)
+        both = split_added(both_pair, after(both_y, carried[1]))
+        two_1 = after(two_1, both[0])
         core_two_1 = lax.ppermute(two_1, BOTH, CORE_HOP)
-        both = both_pair + after(both_y, two_1)
-        decay_grad = rate_pair + after(rate_z2, two_1)
         down_grad, hidden_grad = expert_call(
-            1, 2, widths[0], widths[1], [held_1, two_1, core_1, after(core_two_1, both, decay_grad)],
-            hidden_saved, None, w_down, carried,
+            1, 2, widths[0], widths[1], [held_1, two_1, core_1, core_two_1],
+            hidden_saved, more_w[0], w_down, carried,
         )
     else:
         both = butterfly_sum(both, "exp")

time: 94.9 us -> 90.1 us (0.949)
  waiting for transfers between devices: 26.2 us -> 13.4 us
  starting transfers between devices: 23 us -> 28.8 us
  Pallas kernels: 43 us -> 46.1 us
  other arithmetic: 1.1 us -> 0 us
    ppermute x5 -> x3, waiting for transfers between devices: 12.6 us -> 1.3 us  [exchanged_seeds(): other = lax.ppermute(sent, 'ctx', [(i, i ^ bit) for i in range(count)])]
    ppermute x1, waiting for transfers between devices: 7.14 us -> 0.01 us  [body(): one_1 = lax.ppermute(held_1, BOTH, PLANE_ONE)]
    ppermute x6 -> x9, starting transfers between devices: 9.6 us -> 15.3 us  [z_hops(): return [lax.ppermute(value, BOTH, hop) for hop in Z_HOPS]]
    pallas_call x2, Pallas kernels: 0.1 us -> 2.42 us  [exchanged_seeds(): pl.pallas_call(functools.partial(first_fold_kernel if later is None else...]
    ppermute x1, waiting for transfers between devices: 0.01 us -> 2.23 us  [body(): both_x = lax.ppermute(both, 'exp', [(i, i ^ 1) for i in range(4)])]
    ppermute x1, waiting for transfers between devices: 0.01 us -> 1.93 us  [body(): core_two_1 = lax.ppermute(two_1, BOTH, CORE_HOP)]
    pallas_call x2, Pallas kernels: 25.2 us -> 23.3 us  [expert_call(): pl.pallas_call(functools.partial(expert_kernel, first, last, at, width, o...]
    pallas_call x3, Pallas kernels: 16.5 us -> 18.3 us  [call(): pl.pallas_call(kernel if kernel is seed_kernel else functools.partial(ker...]
  transfers between devices with their start and end apart: 22 -> 23, of which waited for: 10 -> 9; matrix products, arithmetic and copies ran while one was open for 2% -> 1% of each run, Pallas kernels for 27% -> 32%
where the time goes in v1:
time: 90.1 us; the launch traced here: 89.7 us
  Pallas kernels  46.1 us (51%)
  starting transfers between devices  28.8 us (32%)
  waiting for transfers between devices  13.4 us (15%)
    pallas_call x2, Pallas kernels, expert_call(): pl.pallas_call(functools.partial(expert_kernel, first, last, at, width, o...  23.3 us
    pallas_call x3, Pallas kernels, call(): pl.pallas_call(kernel if kernel is seed_kernel else functools.partial(ker...  18.3 us
    ppermute x9, starting transfers between devices, z_hops(): return [lax.ppermute(value, BOTH, hop) for hop in Z_HOPS]  15.3 us
    ppermute x3, starting transfers between devices, exchanged_seeds(): other = lax.ppermute(sent, 'ctx', [(i, i ^ bit) for i in range(count)])  4.42 us
    ppermute x9, waiting for transfers between devices, z_hops(): return [lax.ppermute(value, BOTH, hop) for hop in Z_HOPS]  4.26 us
    pallas_call x2, Pallas kernels, exchanged_seeds(): pl.pallas_call(functools.partial(first_fold_kernel if later is None else...  2.42 us
    ppermute x1, waiting for transfers between devices, body(): both_x = lax.ppermute(both, 'exp', [(i, i ^ 1) for i in range(4)])  2.23 us
    ppermute x1, starting transfers between devices, body(): both_y = lax.ppermute(both_pair, 'exp', [(i, i ^ 2) for i in range(4)])  2 us
  transfers between devices with their start and end apart: 23, of which 9 were waited for; matrix products, arithmetic and copies ran while one was open for 1% of the time, Pallas kernels for 32%

profile of v1, /device:TPU:0, one launch (start us, length us, event | category | flops | bytes accessed | tf_op | source)
XLA Modules:
  0.0 89.7 jit_solution(2725855044355202024)
XLA Ops:
  0.6 3.7 %seed_scan.1 = (f32[17,1024]{1,0:T(8,128)S(1)}, f32[128,1024]{1,0:T(8,128)S(1)}, f32[128,1024]{1,0:T(8,128)S(1)}, f32[128,1024]{1,0:T(8,128)S(1)}, f32[128,1024]{1,0:T(8,128)S(1)}) custom-call(bf16[128,1024]{1,0:T(8,128)(2,1)} %step_ref.1, bf16[128,1024]{1,0:T(8,128)(2,1)} %inp_ref.1, bf16[128,1024]{1,0:T(8,128)(2,1)} %grad_ref.2, f32[16,1024]{1,0:T(8,128)} %rate_ref.9, ...), custom_call_target="tpu_custom_call" | custom-call | tf_op jit(solution)/shard_map/seed_scan/pallas_call | solution.py:354
  4.3 1.2 %pack_tokens.1 = (bf16[32,2176]{1,0:T(8,128)(2,1)S(1)}, bf16[32,2048]{1,0:T(8,128)(2,1)S(1)}) custom-call(bf16[32,4096]{1,0:T(8,128)(2,1)} %grad_ref.3, s32[2,32]{1,0:T(2,128)} %bitcast.3, f32[2,32]{1,0:T(2,128)} %bitcast.4), custom_call_target="tpu_custom_call" | custom-call | tf_op jit(solution)/shard_map/pack_tokens/pallas_call | solution.py:434
  5.6 5.1 %collective-permute-start.4 = (bf16[32,2176]{1,0:T(8,128)(2,1)S(1)}, bf16[32,2176]{1,0:T(8,128)(2,1)S(1)}, u32[]{:S(2)}, u32[]{:S(2)}) collective-permute-start(bf16[32,2176]{1,0:T(8,128)(2,1)S(1)} %get-tuple-element.61.refs_0_), channel_id=1, source_target_pairs={{0,24},{1,25},{2,26},{3,27},{4,28},{5,29},{6,30},{7,31},{8,16},{9,... | collective-permute-start | bytes 417800 | tf_op jit(solution)/shard_map/ppermute | solution.py:463
  10.6 0.0 collective-permute-start.3
  10.6 0.6 collective-permute-start.2
  11.2 0.0 collective-permute-start
  11.2 1.3 %collective-permute-done.other_ref = f32[17,1024]{1,0:T(8,128)S(1)} collective-permute-done((f32[17,1024]{1,0:T(8,128)S(1)}, f32[17,1024]{1,0:T(8,128)S(1)}, u32[]{:S(2)}, u32[]{:S(2)}) %collective-permute-start) | collective-permute-done | bytes 69664 | tf_op jit(solution)/shard_map/ppermute | solution.py:289
  12.5 0.9 fold_1.1
  13.4 1.5 %collective-permute-start.1 = (bf16[18,1024]{1,0:T(8,128)(2,1)S(1)}, bf16[18,1024]{1,0:T(8,128)(2,1)S(1)}, u32[]{:S(2)}, u32[]{:S(2)}) collective-permute-start(bf16[18,1024]{1,0:T(8,128)(2,1)S(1)} %get-tuple-element.65), channel_id=1, source_target_pairs={{0,8},{4,12},{8,0},{12,4},{16,24},{20,28},{24,16},{28,20},{1,9},{5... | collective-permute-start | bytes 110600 | tf_op jit(solution)/shard_map/ppermute | solution.py:289
  14.9 6.2 %forward_scan.1 = (bf16[2048,1024]{1,0:T(8,128)(2,1)S(1)}, f32[16,128]{1,0:T(8,128)S(1)}, bf16[4,896,2048]{2,1,0:T(8,128)(2,1)S(1)}) custom-call(f32[128,1024]{1,0:T(8,128)S(1)} %get-tuple-element.54.step_v, f32[128,1024]{1,0:T(8,128)S(1)} %get-tuple-element.55.drive_v, f32[128,1024]{1,0:T(8,128)S(1)} %get-tuple-element.57.grad_v, f32[16,1024]{1,0:T(8,128)} %rate_ref.9, ...), custom_call_target="tpu_custom_call" | custom-call | tf_op jit(solution)/shard_map/forward_scan/pallas_call | solution.py:354
  21.1 0.0 collective-permute-done.1.other_ref
  21.1 1.5 %fold_2.1 = (f32[17,1024]{1,0:T(8,128)}, f32[17,1024]{1,0:T(8,128)S(1)}, bf16[18,1024]{1,0:T(8,128)(2,1)S(1)}) custom-call(f32[17,1024]{1,0:T(8,128)S(1)} %get-tuple-element.59.total_ref, f32[17,1024]{1,0:T(8,128)S(1)} %get-tuple-element.64.later_ref, bf16[18,1024]{1,0:T(8,128)(2,1)S(1)} %collective-permute-done.1.other_ref, f32[16,1024]{1,0:T(8,128)} %rate_ref.9), custom_call_target="tpu_custom_call" | custom-call | tf_op jit(solution)/shard_map/fold_2/pallas_call | solution.py:293
  22.6 0.0 collective-permute-done.4.refs_3_
  22.6 0.0 collective-permute-done.3.refs_2_
  22.6 0.0 collective-permute-done.2.refs_1_
  22.7 1.6 %collective-permute-start.5 = (bf16[4,32,2176]{2,1,0:T(8,128)(2,1)S(1)}, bf16[4,32,2176]{2,1,0:T(8,128)(2,1)S(1)}, u32[]{:S(2)}, u32[]{:S(2)}) collective-permute-start(bf16[4,32,2176]{2,1,0:T(8,128)(2,1)S(1)} %join_z.2.held_ref), channel_id=1, source_target_pairs={{0,1},{1,0},{2,3},{3,2},{4,6},{5,7},{6,4},{7,5},{8,9},{9,8},{10,11... | collective-permute-start | bytes 1671176 | tf_op jit(solution)/shard_map/ppermute | solution.py:767
  24.2 2.9 %collective-permute-start.6 = (bf16[18,1024]{1,0:T(8,128)(2,1)S(1)}, bf16[18,1024]{1,0:T(8,128)(2,1)S(1)}, u32[]{:S(2)}, u32[]{:S(2)}) collective-permute-start(bf16[18,1024]{1,0:T(8,128)(2,1)S(1)} %get-tuple-element.72), channel_id=1, source_target_pairs={{0,16},{4,20},{8,24},{12,28},{16,0},{20,4},{24,8},{28,12},{1,17},{... | collective-permute-start | bytes 110600 | tf_op jit(solution)/shard_map/ppermute | solution.py:289
  27.2 1.5 %collective-permute-start.13 = (bf16[32,2048]{1,0:T(8,128)(2,1)S(1)}, bf16[32,2048]{1,0:T(8,128)(2,1)S(1)}, u32[]{:S(2)}, u32[]{:S(2)}) collective-permute-start(bf16[32,2048]{1,0:T(8,128)(2,1)S(1)} %get-tuple-element.81.refs_0_), channel_id=1, source_target_pairs={{0,24},{1,25},{2,26},{3,27},{4,28},{5,29},{6,30},{7,31},{8,16},{9,... | collective-permute-start | bytes 393224 | tf_op jit(solution)/shard_map/ppermute | solution.py:463
  28.6 0.0 collective-permute-start.12
  28.6 2.9 %collective-permute-start.11 = (bf16[32,2048]{1,0:T(8,128)(2,1)S(1)}, bf16[32,2048]{1,0:T(8,128)(2,1)S(1)}, u32[]{:S(2)}, u32[]{:S(2)}) collective-permute-start(bf16[32,2048]{1,0:T(8,128)(2,1)S(1)} %get-tuple-element.81.refs_0_), channel_id=1, source_target_pairs={{0,8},{1,9},{2,10},{3,11},{4,12},{5,13},{6,14},{7,15},{8,0},{9,1},... | collective-permute-start | bytes 393224 | tf_op jit(solution)/shard_map/ppermute | solution.py:463
  31.5 0.0 collective-permute-done.6.other_ref
  31.5 0.7 collective-permute-done.5.received_ref
  32.3 0.1 join_plane.2.refs_0_
  32.4 1.6 %collective-permute-start.10 = (bf16[256,2176]{1,0:T(8,128)(2,1)S(1)}, bf16[256,2176]{1,0:T(8,128)(2,1)S(1)}, u32[]{:S(2)}, u32[]{:S(2)}) collective-permute-start(bf16[256,2176]{1,0:T(8,128)(2,1)S(1)} %join_plane.2.refs_0_), channel_id=1, source_target_pairs={{0,2},{1,3},{2,0},{3,1},{4,5},{5,4},{6,7},{7,6},{8,10},{9,11},{10,... | collective-permute-start | bytes 3342344 | tf_op jit(solution)/shard_map/ppermute | solution.py:771
  33.9 8.5 %adjoint_scan.1 = (bf16[128,1024]{1,0:T(8,128)(2,1)}, bf16[128,1024]{1,0:T(8,128)(2,1)}, f32[2,16,128]{2,1,0:T(8,128)S(1)}, f32[16,1024]{1,0:T(8,128)S(1)}, bf16[3,896,2048]{2,1,0:T(8,128)(2,1)S(1)}) custom-call(f32[128,1024]{1,0:T(8,128)S(1)} %get-tuple-element.54.step_v, f32[128,1024]{1,0:T(8,128)S(1)} %get-tuple-element.55.drive_v, ...), custom_call_target="tpu_custom_call" | custom-call | flops 13799999488 | tf_op jit(solution)/shard_map/adjoint_scan/pallas_call | solution.py:354
  42.4 0.0 copy-start
  42.5 0.1 collective-permute-start.8
  42.5 1.2 %collective-permute-done.8.two_ref = f32[16,1024]{1,0:T(8,128)S(1)} collective-permute-done((f32[16,1024]{1,0:T(8,128)S(1)}, f32[16,1024]{1,0:T(8,128)S(1)}, u32[]{:S(2)}, u32[]{:S(2)}) %collective-permute-start.8) | collective-permute-done | bytes 65568 | tf_op jit(solution)/shard_map/ppermute | solution.py:787
  43.8 1.5 %collective-permute-start.7 = (f32[2,16,128]{2,1,0:T(8,128)S(1)}, f32[2,16,128]{2,1,0:T(8,128)S(1)}, u32[]{:S(2)}, u32[]{:S(2)}) collective-permute-start(f32[2,16,128]{2,1,0:T(8,128)S(1)} %get-tuple-element.77.one_ref), channel_id=1, source_target_pairs={{0,1},{1,0},{2,3},{3,2},{4,5},{5,4},{6,7},{7,6},{8,9},{9,8},{10,11... | collective-permute-start | bytes 49160 | tf_op jit(solution)/shard_map/ppermute | solution.py:788
  45.3 2.2 %collective-permute-done.7.two_ref = f32[2,16,128]{2,1,0:T(8,128)S(1)} collective-permute-done((f32[2,16,128]{2,1,0:T(8,128)S(1)}, f32[2,16,128]{2,1,0:T(8,128)S(1)}, u32[]{:S(2)}, u32[]{:S(2)}) %collective-permute-start.7) | collective-permute-done | bytes 16416 | tf_op jit(solution)/shard_map/ppermute | solution.py:788
  47.5 0.0 collective-permute-done.13.refs_3_
  47.5 0.0 collective-permute-done.12.refs_2_
  47.5 0.0 collective-permute-done.11.refs_1_
  47.6 1.6 %collective-permute-start.19 = (bf16[4,32,2048]{2,1,0:T(8,128)(2,1)S(1)}, bf16[4,32,2048]{2,1,0:T(8,128)(2,1)S(1)}, u32[]{:S(2)}, u32[]{:S(2)}) collective-permute-start(bf16[4,32,2048]{2,1,0:T(8,128)(2,1)S(1)} %join_z.3.held_ref), channel_id=1, source_target_pairs={{0,1},{1,0},{2,3},{3,2},{4,6},{5,7},{6,4},{7,5},{8,9},{9,8},{10,11... | collective-permute-start | bytes 1572872 | tf_op jit(solution)/shard_map/ppermute | solution.py:793
  49.2 4.7 %collective-permute-start.16 = (bf16[16,1024]{1,0:T(8,128)(2,1)S(1)}, bf16[16,1024]{1,0:T(8,128)(2,1)S(1)}, u32[]{:S(2)}, u32[]{:S(2)}) collective-permute-start(bf16[16,1024]{1,0:T(8,128)(2,1)S(1)} %add_two.2.a_ref), channel_id=1, source_target_pairs={{0,24},{1,25},{2,26},{3,27},{4,28},{5,29},{6,30},{7,31},{8,16},{9,... | collective-permute-start | bytes 98312 | tf_op jit(solution)/shard_map/ppermute | solution.py:463
  53.9 0.0 collective-permute-start.15
  53.9 0.6 collective-permute-start.14
  54.5 1.4 %collective-permute-done.16.d_ref = bf16[16,1024]{1,0:T(8,128)(2,1)S(1)} collective-permute-done((bf16[16,1024]{1,0:T(8,128)(2,1)S(1)}, bf16[16,1024]{1,0:T(8,128)(2,1)S(1)}, u32[]{:S(2)}, u32[]{:S(2)}) %collective-permute-start.16) | collective-permute-done | bytes 32800 | tf_op jit(solution)/shard_map/ppermute | solution.py:463
  55.9 2.8 %collective-permute-done.15.c_ref = bf16[16,1024]{1,0:T(8,128)(2,1)S(1)} collective-permute-done((bf16[16,1024]{1,0:T(8,128)(2,1)S(1)}, bf16[16,1024]{1,0:T(8,128)(2,1)S(1)}, u32[]{:S(2)}, u32[]{:S(2)}) %collective-permute-start.15) | collective-permute-done | bytes 32800 | tf_op jit(solution)/shard_map/ppermute | solution.py:463
  58.7 0.0 collective-permute-done.14.b_ref
  58.7 0.0 collective-permute-done.10.refs_1_
  58.7 0.1 collective-permute-start.18
  58.8 0.5 collective-permute-start.17
  59.3 0.0 collective-permute-done.19.received_ref
  59.3 0.1 join_plane.3.refs_0_
  59.4 0.1 collective-permute-start.20
  59.5 2.0 %collective-permute-start.9 = (f32[2,16,128]{2,1,0:T(8,128)S(1)}, f32[2,16,128]{2,1,0:T(8,128)S(1)}, u32[]{:S(2)}, u32[]{:S(2)}) collective-permute-start(f32[2,16,128]{2,1,0:T(8,128)S(1)} %add_two.3.one_ref), channel_id=1, source_target_pairs={{0,2},{1,3},{2,0},{3,1},{4,6},{5,7},{6,4},{7,5},{8,10},{9,11},{10,... | collective-permute-start | bytes 49160 | tf_op jit(solution)/shard_map/ppermute | solution.py:791
  61.5 0.0 collective-permute-start.21
  61.5 0.1 collective-permute-done.18.refs_3_
  61.6 1.6 %collective-permute-done.17.refs_2_ = bf16[256,2176]{1,0:T(8,128)(2,1)S(1)} collective-permute-done((bf16[256,2176]{1,0:T(8,128)(2,1)S(1)}, bf16[256,2176]{1,0:T(8,128)(2,1)S(1)}, u32[]{:S(2)}, u32[]{:S(2)}) %collective-permute-start.17) | collective-permute-done | bytes 1114144 | tf_op jit(solution)/shard_map/ppermute | solution.py:772
  63.1 0.0 copy-done
  63.1 11.2 %experts_0.1 = (bf16[4,896,4096]{2,1,0:T(8,128)(2,1)}, f32[4,256,896]{2,1,0:T(8,128)S(1)}, bf16[4,256,256]{2,1,0:T(8,128)(2,1)S(1)}, f32[4,256,128]{2,1,0:T(8,128)S(1)}) custom-call(bf16[256,2176]{1,0:T(8,128)(2,1)S(1)} %join_plane.2.refs_0_, bf16[256,2176]{1,0:T(8,128)(2,1)S(1)} %collective-permute-done.10.refs_1_, ...), custom_call_target="tpu_custom_call" | custom-call | tf_op jit(solution)/shard_map/experts_0/pallas_call | solution.py:691
  74.4 0.0 collective-permute-done.9.two_ref
  74.4 0.6 split_add.1
  75.0 0.0 collective-permute-done.20.refs_1_
  75.0 0.1 collective-permute-start.22
  75.1 0.6 copy.23
  75.8 0.0 collective-permute-done.21.refs_2_
  75.8 1.9 %collective-permute-done.22.refs_3_ = bf16[256,2048]{1,0:T(8,128)(2,1)S(1)} collective-permute-done((bf16[256,2048]{1,0:T(8,128)(2,1)S(1)}, bf16[256,2048]{1,0:T(8,128)(2,1)S(1)}, u32[]{:S(2)}, u32[]{:S(2)}) %collective-permute-start.22) | collective-permute-done | bytes 1048608 | tf_op jit(solution)/shard_map/ppermute | solution.py:807
  77.7 12.0 %experts_1.1 = (bf16[4,896,4096]{2,1,0:T(8,128)(2,1)}, bf16[4,256,896]{2,1,0:T(8,128)(2,1)}) custom-call(bf16[256,2048]{1,0:T(8,128)(2,1)S(1)} %join_plane.3.refs_0_, bf16[256,2048]{1,0:T(8,128)(2,1)S(1)} %collective-permute-done.20.refs_1_, bf16[256,2048]{1,0:T(8,128)(2,1)S(1)} %collective-permute-done.21.refs_2_, ...), custom_call_target="tpu_custom_call", output_to_operand_aliasing={{0}: (10, {})} | custom-call | tf_op jit(solution)/shard_map/experts_1/pallas_call | solution.py:691
  (5 shorter events, 0.1 us)
Async XLA Ops:
  5.6 17.1 %collective-permute-start.4 = (bf16[32,2176]{1,0:T(8,128)(2,1)S(1)}, bf16[32,2176]{1,0:T(8,128)(2,1)S(1)}, u32[]{:S(2)}, u32[]{:S(2)}) collective-permute-start(bf16[32,2176]{1,0:T(8,128)(2,1)S(1)} %get-tuple-element.61.refs_0_), channel_id=1, source_target_pairs={{0,24},{1,25},{2,26},{3,27},{4,28},{5,29},{6,30},{7,31},{8,16},{9,... | collective-permute-start | bytes 417800 | tf_op jit(solution)/shard_map/ppermute | solution.py:463
  10.6 12.0 %collective-permute-start.3 = (bf16[32,2176]{1,0:T(8,128)(2,1)S(1)}, bf16[32,2176]{1,0:T(8,128)(2,1)S(1)}, u32[]{:S(2)}, u32[]{:S(2)}) collective-permute-start(bf16[32,2176]{1,0:T(8,128)(2,1)S(1)} %get-tuple-element.61.refs_0_), channel_id=1, source_target_pairs={{0,16},{1,17},{2,18},{3,19},{4,20},{5,21},{6,22},{7,23},{8,24},{9,... | collective-permute-start | bytes 417800 | tf_op jit(solution)/shard_map/ppermute | solution.py:463
  10.6 12.0 %collective-permute-start.2 = (bf16[32,2176]{1,0:T(8,128)(2,1)S(1)}, bf16[32,2176]{1,0:T(8,128)(2,1)S(1)}, u32[]{:S(2)}, u32[]{:S(2)}) collective-permute-start(bf16[32,2176]{1,0:T(8,128)(2,1)S(1)} %get-tuple-element.61.refs_0_), channel_id=1, source_target_pairs={{0,8},{1,9},{2,10},{3,11},{4,12},{5,13},{6,14},{7,15},{8,0},{9,1},... | collective-permute-start | bytes 417800 | tf_op jit(solution)/shard_map/ppermute | solution.py:463
  11.2 1.3 %collective-permute-start = (f32[17,1024]{1,0:T(8,128)S(1)}, f32[17,1024]{1,0:T(8,128)S(1)}, u32[]{:S(2)}, u32[]{:S(2)}) collective-permute-start(f32[17,1024]{1,0:T(8,128)S(1)} %get-tuple-element.58.total_ref), channel_id=1, source_target_pairs={{0,4},{4,0},{8,12},{12,8},{16,20},{20,16},{24,28},{28,24},{1,5},{5... | collective-permute-start | bytes 208904 | tf_op jit(solution)/shard_map/ppermute | solution.py:289
  13.4 7.7 %collective-permute-start.1 = (bf16[18,1024]{1,0:T(8,128)(2,1)S(1)}, bf16[18,1024]{1,0:T(8,128)(2,1)S(1)}, u32[]{:S(2)}, u32[]{:S(2)}) collective-permute-start(bf16[18,1024]{1,0:T(8,128)(2,1)S(1)} %get-tuple-element.65), channel_id=1, source_target_pairs={{0,8},{4,12},{8,0},{12,4},{16,24},{20,28},{24,16},{28,20},{1,9},{5... | collective-permute-start | bytes 110600 | tf_op jit(solution)/shard_map/ppermute | solution.py:289
  22.7 9.6 %collective-permute-start.5 = (bf16[4,32,2176]{2,1,0:T(8,128)(2,1)S(1)}, bf16[4,32,2176]{2,1,0:T(8,128)(2,1)S(1)}, u32[]{:S(2)}, u32[]{:S(2)}) collective-permute-start(bf16[4,32,2176]{2,1,0:T(8,128)(2,1)S(1)} %join_z.2.held_ref), channel_id=1, source_target_pairs={{0,1},{1,0},{2,3},{3,2},{4,6},{5,7},{6,4},{7,5},{8,9},{9,8},{10,11... | collective-permute-start | bytes 1671176 | tf_op jit(solution)/shard_map/ppermute | solution.py:767
  24.2 7.3 %collective-permute-start.6 = (bf16[18,1024]{1,0:T(8,128)(2,1)S(1)}, bf16[18,1024]{1,0:T(8,128)(2,1)S(1)}, u32[]{:S(2)}, u32[]{:S(2)}) collective-permute-start(bf16[18,1024]{1,0:T(8,128)(2,1)S(1)} %get-tuple-element.72), channel_id=1, source_target_pairs={{0,16},{4,20},{8,24},{12,28},{16,0},{20,4},{24,8},{28,12},{1,17},{... | collective-permute-start | bytes 110600 | tf_op jit(solution)/shard_map/ppermute | solution.py:289
  27.2 20.4 %collective-permute-start.13 = (bf16[32,2048]{1,0:T(8,128)(2,1)S(1)}, bf16[32,2048]{1,0:T(8,128)(2,1)S(1)}, u32[]{:S(2)}, u32[]{:S(2)}) collective-permute-start(bf16[32,2048]{1,0:T(8,128)(2,1)S(1)} %get-tuple-element.81.refs_0_), channel_id=1, source_target_pairs={{0,24},{1,25},{2,26},{3,27},{4,28},{5,29},{6,30},{7,31},{8,16},{9,... | collective-permute-start | bytes 393224 | tf_op jit(solution)/shard_map/ppermute | solution.py:463
  28.6 18.9 %collective-permute-start.12 = (bf16[32,2048]{1,0:T(8,128)(2,1)S(1)}, bf16[32,2048]{1,0:T(8,128)(2,1)S(1)}, u32[]{:S(2)}, u32[]{:S(2)}) collective-permute-start(bf16[32,2048]{1,0:T(8,128)(2,1)S(1)} %get-tuple-element.81.refs_0_), channel_id=1, source_target_pairs={{0,16},{1,17},{2,18},{3,19},{4,20},{5,21},{6,22},{7,23},{8,24},{9,... | collective-permute-start | bytes 393224 | tf_op jit(solution)/shard_map/ppermute | solution.py:463
  28.6 18.9 %collective-permute-start.11 = (bf16[32,2048]{1,0:T(8,128)(2,1)S(1)}, bf16[32,2048]{1,0:T(8,128)(2,1)S(1)}, u32[]{:S(2)}, u32[]{:S(2)}) collective-permute-start(bf16[32,2048]{1,0:T(8,128)(2,1)S(1)} %get-tuple-element.81.refs_0_), channel_id=1, source_target_pairs={{0,8},{1,9},{2,10},{3,11},{4,12},{5,13},{6,14},{7,15},{8,0},{9,1},... | collective-permute-start | bytes 393224 | tf_op jit(solution)/shard_map/ppermute | solution.py:463
  32.4 26.4 %collective-permute-start.10 = (bf16[256,2176]{1,0:T(8,128)(2,1)S(1)}, bf16[256,2176]{1,0:T(8,128)(2,1)S(1)}, u32[]{:S(2)}, u32[]{:S(2)}) collective-permute-start(bf16[256,2176]{1,0:T(8,128)(2,1)S(1)} %join_plane.2.refs_0_), channel_id=1, source_target_pairs={{0,2},{1,3},{2,0},{3,1},{4,5},{5,4},{6,7},{7,6},{8,10},{9,11},{10,... | collective-permute-start | bytes 3342344 | tf_op jit(solution)/shard_map/ppermute | solution.py:771
  42.4 20.7 %copy-start = (bf16[4,256,896]{2,1,0:T(8,128)(2,1)S(1)}, bf16[4,256,896]{2,1,0:T(8,128)(2,1)}, u32[]{:S(2)}) copy-start(bf16[4,256,896]{2,1,0:T(8,128)(2,1)} %refs_4_.3) | copy-start | bytes 5505028
  42.5 1.3 %collective-permute-start.8 = (f32[16,1024]{1,0:T(8,128)S(1)}, f32[16,1024]{1,0:T(8,128)S(1)}, u32[]{:S(2)}, u32[]{:S(2)}) collective-permute-start(f32[16,1024]{1,0:T(8,128)S(1)} %get-tuple-element.78.one_ref), channel_id=1, source_target_pairs={{0,4},{1,5},{2,6},{3,7},{4,0},{5,1},{6,2},{7,3},{8,12},{9,13},{10,... | collective-permute-start | bytes 196616 | tf_op jit(solution)/shard_map/ppermute | solution.py:787
  43.8 3.7 %collective-permute-start.7 = (f32[2,16,128]{2,1,0:T(8,128)S(1)}, f32[2,16,128]{2,1,0:T(8,128)S(1)}, u32[]{:S(2)}, u32[]{:S(2)}) collective-permute-start(f32[2,16,128]{2,1,0:T(8,128)S(1)} %get-tuple-element.77.one_ref), channel_id=1, source_target_pairs={{0,1},{1,0},{2,3},{3,2},{4,5},{5,4},{6,7},{7,6},{8,9},{9,8},{10,11... | collective-permute-start | bytes 49160 | tf_op jit(solution)/shard_map/ppermute | solution.py:788
  47.6 11.7 %collective-permute-start.19 = (bf16[4,32,2048]{2,1,0:T(8,128)(2,1)S(1)}, bf16[4,32,2048]{2,1,0:T(8,128)(2,1)S(1)}, u32[]{:S(2)}, u32[]{:S(2)}) collective-permute-start(bf16[4,32,2048]{2,1,0:T(8,128)(2,1)S(1)} %join_z.3.held_ref), channel_id=1, source_target_pairs={{0,1},{1,0},{2,3},{3,2},{4,6},{5,7},{6,4},{7,5},{8,9},{9,8},{10,11... | collective-permute-start | bytes 1572872 | tf_op jit(solution)/shard_map/ppermute | solution.py:793
  49.2 6.7 %collective-permute-start.16 = (bf16[16,1024]{1,0:T(8,128)(2,1)S(1)}, bf16[16,1024]{1,0:T(8,128)(2,1)S(1)}, u32[]{:S(2)}, u32[]{:S(2)}) collective-permute-start(bf16[16,1024]{1,0:T(8,128)(2,1)S(1)} %add_two.2.a_ref), channel_id=1, source_target_pairs={{0,24},{1,25},{2,26},{3,27},{4,28},{5,29},{6,30},{7,31},{8,16},{9,... | collective-permute-start | bytes 98312 | tf_op jit(solution)/shard_map/ppermute | solution.py:463
  53.9 4.8 %collective-permute-start.15 = (bf16[16,1024]{1,0:T(8,128)(2,1)S(1)}, bf16[16,1024]{1,0:T(8,128)(2,1)S(1)}, u32[]{:S(2)}, u32[]{:S(2)}) collective-permute-start(bf16[16,1024]{1,0:T(8,128)(2,1)S(1)} %add_two.2.a_ref), channel_id=1, source_target_pairs={{0,16},{1,17},{2,18},{3,19},{4,20},{5,21},{6,22},{7,23},{8,24},{9,... | collective-permute-start | bytes 98312 | tf_op jit(solution)/shard_map/ppermute | solution.py:463
  53.9 4.8 %collective-permute-start.14 = (bf16[16,1024]{1,0:T(8,128)(2,1)S(1)}, bf16[16,1024]{1,0:T(8,128)(2,1)S(1)}, u32[]{:S(2)}, u32[]{:S(2)}) collective-permute-start(bf16[16,1024]{1,0:T(8,128)(2,1)S(1)} %add_two.2.a_ref), channel_id=1, source_target_pairs={{0,8},{1,9},{2,10},{3,11},{4,12},{5,13},{6,14},{7,15},{8,0},{9,1},... | collective-permute-start | bytes 98312 | tf_op jit(solution)/shard_map/ppermute | solution.py:463
  58.7 2.8 %collective-permute-start.18 = (bf16[256,2176]{1,0:T(8,128)(2,1)S(1)}, bf16[256,2176]{1,0:T(8,128)(2,1)S(1)}, u32[]{:S(2)}, u32[]{:S(2)}) collective-permute-start(bf16[256,2176]{1,0:T(8,128)(2,1)S(1)} %collective-permute-done.10.refs_1_), channel_id=1, source_target_pairs={{0,4},{1,5},{2,6},{3,7},{4,0},{5,1},{6,2},{7,3},{8,12},{9,13},{10,... | collective-permute-start | bytes 3342344 | tf_op jit(solution)/shard_map/ppermute | solution.py:797
  58.8 4.3 %collective-permute-start.17 = (bf16[256,2176]{1,0:T(8,128)(2,1)S(1)}, bf16[256,2176]{1,0:T(8,128)(2,1)S(1)}, u32[]{:S(2)}, u32[]{:S(2)}) collective-permute-start(bf16[256,2176]{1,0:T(8,128)(2,1)S(1)} %join_plane.2.refs_0_), channel_id=1, source_target_pairs={{0,4},{1,5},{2,6},{3,7},{4,0},{5,1},{6,2},{7,3},{8,12},{9,13},{10,... | collective-permute-start | bytes 3342344 | tf_op jit(solution)/shard_map/ppermute | solution.py:772
  59.4 15.6 %collective-permute-start.20 = (bf16[256,2048]{1,0:T(8,128)(2,1)S(1)}, bf16[256,2048]{1,0:T(8,128)(2,1)S(1)}, u32[]{:S(2)}, u32[]{:S(2)}) collective-permute-start(bf16[256,2048]{1,0:T(8,128)(2,1)S(1)} %join_plane.3.refs_0_), channel_id=1, source_target_pairs={{0,2},{1,3},{2,0},{3,1},{4,5},{5,4},{6,7},{7,6},{8,10},{9,11},{10,... | collective-permute-start | bytes 3145736 | tf_op jit(solution)/shard_map/ppermute | solution.py:799
  59.5 14.9 %collective-permute-start.9 = (f32[2,16,128]{2,1,0:T(8,128)S(1)}, f32[2,16,128]{2,1,0:T(8,128)S(1)}, u32[]{:S(2)}, u32[]{:S(2)}) collective-permute-start(f32[2,16,128]{2,1,0:T(8,128)S(1)} %add_two.3.one_ref), channel_id=1, source_target_pairs={{0,2},{1,3},{2,0},{3,1},{4,6},{5,7},{6,4},{7,5},{8,10},{9,11},{10,... | collective-permute-start | bytes 49160 | tf_op jit(solution)/shard_map/ppermute | solution.py:791
  61.5 14.3 %collective-permute-start.21 = (bf16[256,2048]{1,0:T(8,128)(2,1)S(1)}, bf16[256,2048]{1,0:T(8,128)(2,1)S(1)}, u32[]{:S(2)}, u32[]{:S(2)}) collective-permute-start(bf16[256,2048]{1,0:T(8,128)(2,1)S(1)} %join_plane.3.refs_0_), channel_id=1, source_target_pairs={{0,4},{1,5},{2,6},{3,7},{4,0},{5,1},{6,2},{7,3},{8,12},{9,13},{10,... | collective-permute-start | bytes 3145736 | tf_op jit(solution)/shard_map/ppermute | solution.py:800
  75.0 2.7 %collective-permute-start.22 = (bf16[256,2048]{1,0:T(8,128)(2,1)S(1)}, bf16[256,2048]{1,0:T(8,128)(2,1)S(1)}, u32[]{:S(2)}, u32[]{:S(2)}) collective-permute-start(bf16[256,2048]{1,0:T(8,128)(2,1)S(1)} %collective-permute-done.20.refs_1_), channel_id=1, source_target_pairs={{0,4},{1,5},{2,6},{3,7},{4,0},{5,1},{6,2},{7,3},{8,12},{9,13},{10,... | collective-permute-start | bytes 3145736 | tf_op jit(solution)/shard_map/ppermute | solution.py:807

commit v2 on v1

--- a/solution.py
+++ b/solution.py
@@ -463,34 +463,26 @@
     return [lax.ppermute(value, BOTH, hop) for hop in Z_HOPS]
 
 
-def small_call(kernel, name, shape, *operands, dtype=BF16, limit=2 * 1024 * 1024):
+def small_call(kernel, name, shape, *operands, dtype=BF16, limit=2 * 1024 * 1024, result=False):
     kept = pl.BlockSpec(memory_space=pltpu.VMEM)
     return pl.pallas_call(
         kernel,
         name=name,
         in_specs=[kept] * len(operands),
         out_specs=kept,
-        out_shape=pltpu.VMEM(shape, dtype),
+        out_shape=(jax.ShapeDtypeStruct if result else pltpu.VMEM)(shape, dtype),
         compiler_params=pltpu.CompilerParams(vmem_limit_bytes=limit),
         cost_estimate=pl.CostEstimate(flops=0, bytes_accessed=0, transcendentals=0),
     )(*(in_vmem(value) for value in operands))
 
 
 def add_kernel(one_ref, two_ref, out_ref):
-    out_ref[...] = (one_ref[...] + two_ref[...]).astype(out_ref.dtype)
-
-
-def added(one, two, dtype=F32):
-    return small_call(add_kernel, "add_two", one.shape, one, two, dtype=dtype)
-
-
-def add_four_kernel(a_ref, b_ref, c_ref, d_ref, out_ref):
-    a, b, c, d = (ref[...].astype(F32) for ref in (a_ref, b_ref, c_ref, d_ref))
-    out_ref[...] = (a + b) + (c + d)
-
-
-def added_four(*values):
-    return small_call(add_four_kernel, "add_four", values[0].shape, *values, dtype=F32)
+    total = one_ref[...].astype(F32) + two_ref[...].astype(F32)
+    out_ref[...] = total.astype(out_ref.dtype)
+
+
+def added(one, two, dtype=F32, result=False):
+    return small_call(add_kernel, "add_two", one.shape, one, two, dtype=dtype, result=result)
 
 
 def split_add_kernel(one_ref, two_ref, first_ref, second_ref):
@@ -791,15 +783,17 @@
         both_y = lax.ppermute(both_pair, "exp", [(i, i ^ 2) for i in range(4)])
         held_1 = join_z(packed[1], [after(value, both_pair) for value in from_z[1]])
         one_1 = lax.ppermute(held_1, BOTH, PLANE_ONE)
-        rate_z = z_hops(after(rate_chip, held_1))
-        decay_grad = added_four(rate_chip, *rate_z)
-        two_0 = after(two_0, decay_grad)
+        rate_z1 = lax.ppermute(after(rate_chip, held_1), BOTH, Z_HOPS[0])
+        rate_pair = added(rate_chip, rate_z1, BF16)
+        rate_z2 = lax.ppermute(rate_pair, BOTH, Z_HOPS[1])
+        two_0 = after(two_0, rate_pair)
         core_two_0 = lax.ppermute(two_0, BOTH, CORE_HOP)
         held_1 = join_plane(held_1, after(one_1, two_0))
+        decay_grad = added(rate_pair, after(rate_z2, held_1), result=True)
         two_1 = lax.ppermute(held_1, BOTH, PLANE_TWO)
         core_1 = lax.ppermute(held_1, BOTH, CORE_HOP)
         carried = expert_call(
-            0, 2, 0, widths[0], [held_0, two_0, core_0, after(core_two_0, held_1)],
+            0, 2, 0, widths[0], [held_0, two_0, core_0, after(core_two_0, decay_grad)],
             hidden_saved, held_w[0], w_down, None,
         )
         both = split_added(both_pair, after(both_y, carried[1]))

time: 90.1 us -> 91.1 us (1.011); the launches traced: 89.7 us -> 89.6 us
    ppermute x9 -> x6, starting transfers between devices: 15.3 us -> 10 us  [z_hops(): return [lax.ppermute(value, BOTH, hop) for hop in Z_HOPS]]
    ppermute x0 -> x2, starting transfers between devices: none -> 4.94 us  [the longest x1 2.92 us: body(): rate_z2 = lax.ppermute(rate_pair, BOTH, Z_HOPS[1])]
    ppermute x9 -> x6, waiting for transfers between devices: 4.26 us -> 0.02 us  [z_hops(): return [lax.ppermute(value, BOTH, hop) for hop in Z_HOPS]]
    ppermute x1, waiting for transfers between devices: 0.01 us -> 3.17 us  [body(): one_1 = lax.ppermute(held_1, BOTH, PLANE_ONE)]
    ppermute x0 -> x2, waiting for transfers between devices: none -> 2.27 us  [the longest x1 1.89 us: body(): rate_z1 = lax.ppermute(after(rate_chip, held_1), BOTH, Z_HOPS[0])]
    ppermute x1, waiting for transfers between devices: 1.59 us -> 0.01 us  [body(): core_0 = lax.ppermute(held_0, BOTH, CORE_HOP)]
  transfers between devices with their start and end apart: 23 -> 22, of which waited for: 9 -> 8; matrix products, arithmetic and copies ran while one was open for 1% -> 0% of each run, Pallas kernels for 32% -> 33%
where the time goes in v2:
time: 91.1 us; the launch traced here: 89.6 us
  Pallas kernels  46.8 us (51%)
  starting transfers between devices  28.8 us (32%)
  waiting for transfers between devices  13.3 us (15%)
    pallas_call x2, Pallas kernels, expert_call(): pl.pallas_call(functools.partial(expert_kernel, first, last, at, width, o...  23.3 us
    pallas_call x3, Pallas kernels, call(): pl.pallas_call(kernel if kernel is seed_kernel else functools.partial(ker...  18.3 us
    ppermute x6, starting transfers between devices, z_hops(): return [lax.ppermute(value, BOTH, hop) for hop in Z_HOPS]  10 us
    ppermute x3, starting transfers between devices, exchanged_seeds(): other = lax.ppermute(sent, 'ctx', [(i, i ^ bit) for i in range(count)])  4.42 us
    ppermute x1, waiting for transfers between devices, body(): one_1 = lax.ppermute(held_1, BOTH, PLANE_ONE)  3.17 us
    ppermute x1, starting transfers between devices, body(): rate_z2 = lax.ppermute(rate_pair, BOTH, Z_HOPS[1])  2.92 us
    pallas_call x2, Pallas kernels, exchanged_seeds(): pl.pallas_call(functools.partial(first_fold_kernel if later is None else...  2.42 us
    ppermute x1, waiting for transfers between devices, body(): core_two_1 = lax.ppermute(two_1, BOTH, CORE_HOP)  2.28 us
  transfers between devices with their start and end apart: 22, of which 8 were waited for; matrix products, arithmetic and copies ran while one was open for 0% of the time, Pallas kernels for 33%

profile of v2, /device:TPU:0, one launch (start us, length us, event | category | flops | bytes accessed | tf_op | source)
XLA Modules:
  0.0 89.6 jit_solution(14282896930758989810)
XLA Ops:
  0.6 3.7 %seed_scan.1 = (f32[17,1024]{1,0:T(8,128)S(1)}, f32[128,1024]{1,0:T(8,128)S(1)}, f32[128,1024]{1,0:T(8,128)S(1)}, f32[128,1024]{1,0:T(8,128)S(1)}, f32[128,1024]{1,0:T(8,128)S(1)}) custom-call(bf16[128,1024]{1,0:T(8,128)(2,1)} %step_ref.1, bf16[128,1024]{1,0:T(8,128)(2,1)} %inp_ref.1, bf16[128,1024]{1,0:T(8,128)(2,1)} %grad_ref.2, f32[16,1024]{1,0:T(8,128)} %rate_ref.9, ...), custom_call_target="tpu_custom_call" | custom-call | tf_op jit(solution)/shard_map/seed_scan/pallas_call | solution.py:354
  4.3 1.2 %pack_tokens.1 = (bf16[32,2176]{1,0:T(8,128)(2,1)S(1)}, bf16[32,2048]{1,0:T(8,128)(2,1)S(1)}) custom-call(bf16[32,4096]{1,0:T(8,128)(2,1)} %grad_ref.3, s32[2,32]{1,0:T(2,128)} %bitcast.3, f32[2,32]{1,0:T(2,128)} %bitcast.4), custom_call_target="tpu_custom_call" | custom-call | tf_op jit(solution)/shard_map/pack_tokens/pallas_call | solution.py:434
  5.5 5.1 %collective-permute-start.4 = (bf16[32,2176]{1,0:T(8,128)(2,1)S(1)}, bf16[32,2176]{1,0:T(8,128)(2,1)S(1)}, u32[]{:S(2)}, u32[]{:S(2)}) collective-permute-start(bf16[32,2176]{1,0:T(8,128)(2,1)S(1)} %get-tuple-element.62.refs_0_), channel_id=1, source_target_pairs={{0,24},{1,25},{2,26},{3,27},{4,28},{5,29},{6,30},{7,31},{8,16},{9,... | collective-permute-start | bytes 417800 | tf_op jit(solution)/shard_map/ppermute | solution.py:463
  10.6 0.0 collective-permute-start.3
  10.6 0.6 collective-permute-start.2
  11.2 0.0 collective-permute-start
  11.2 1.3 %collective-permute-done.other_ref = f32[17,1024]{1,0:T(8,128)S(1)} collective-permute-done((f32[17,1024]{1,0:T(8,128)S(1)}, f32[17,1024]{1,0:T(8,128)S(1)}, u32[]{:S(2)}, u32[]{:S(2)}) %collective-permute-start) | collective-permute-done | bytes 69664 | tf_op jit(solution)/shard_map/ppermute | solution.py:289
  12.5 0.9 fold_1.1
  13.4 1.5 %collective-permute-start.1 = (bf16[18,1024]{1,0:T(8,128)(2,1)S(1)}, bf16[18,1024]{1,0:T(8,128)(2,1)S(1)}, u32[]{:S(2)}, u32[]{:S(2)}) collective-permute-start(bf16[18,1024]{1,0:T(8,128)(2,1)S(1)} %get-tuple-element.66), channel_id=1, source_target_pairs={{0,8},{4,12},{8,0},{12,4},{16,24},{20,28},{24,16},{28,20},{1,9},{5... | collective-permute-start | bytes 110600 | tf_op jit(solution)/shard_map/ppermute | solution.py:289
  14.9 6.2 %forward_scan.1 = (bf16[2048,1024]{1,0:T(8,128)(2,1)S(1)}, f32[16,128]{1,0:T(8,128)S(1)}, bf16[4,896,2048]{2,1,0:T(8,128)(2,1)S(1)}) custom-call(f32[128,1024]{1,0:T(8,128)S(1)} %get-tuple-element.55.step_v, f32[128,1024]{1,0:T(8,128)S(1)} %get-tuple-element.56.drive_v, f32[128,1024]{1,0:T(8,128)S(1)} %get-tuple-element.58.grad_v, f32[16,1024]{1,0:T(8,128)} %rate_ref.9, ...), custom_call_target="tpu_custom_call" | custom-call | tf_op jit(solution)/shard_map/forward_scan/pallas_call | solution.py:354
  21.1 0.0 collective-permute-done.1.other_ref
  21.1 1.5 %fold_2.1 = (f32[17,1024]{1,0:T(8,128)}, f32[17,1024]{1,0:T(8,128)S(1)}, bf16[18,1024]{1,0:T(8,128)(2,1)S(1)}) custom-call(f32[17,1024]{1,0:T(8,128)S(1)} %get-tuple-element.60.total_ref, f32[17,1024]{1,0:T(8,128)S(1)} %get-tuple-element.65.later_ref, bf16[18,1024]{1,0:T(8,128)(2,1)S(1)} %collective-permute-done.1.other_ref, f32[16,1024]{1,0:T(8,128)} %rate_ref.9), custom_call_target="tpu_custom_call" | custom-call | tf_op jit(solution)/shard_map/fold_2/pallas_call | solution.py:293
  22.6 0.0 collective-permute-done.4.refs_3_
  22.6 0.0 collective-permute-done.3.refs_2_
  22.6 0.0 collective-permute-done.2.refs_1_
  22.7 1.6 %collective-permute-start.5 = (bf16[4,32,2176]{2,1,0:T(8,128)(2,1)S(1)}, bf16[4,32,2176]{2,1,0:T(8,128)(2,1)S(1)}, u32[]{:S(2)}, u32[]{:S(2)}) collective-permute-start(bf16[4,32,2176]{2,1,0:T(8,128)(2,1)S(1)} %join_z.2.held_ref), channel_id=1, source_target_pairs={{0,1},{1,0},{2,3},{3,2},{4,6},{5,7},{6,4},{7,5},{8,9},{9,8},{10,11... | collective-permute-start | bytes 1671176 | tf_op jit(solution)/shard_map/ppermute | solution.py:759
  24.2 2.9 %collective-permute-start.6 = (bf16[18,1024]{1,0:T(8,128)(2,1)S(1)}, bf16[18,1024]{1,0:T(8,128)(2,1)S(1)}, u32[]{:S(2)}, u32[]{:S(2)}) collective-permute-start(bf16[18,1024]{1,0:T(8,128)(2,1)S(1)} %get-tuple-element.73), channel_id=1, source_target_pairs={{0,16},{4,20},{8,24},{12,28},{16,0},{20,4},{24,8},{28,12},{1,17},{... | collective-permute-start | bytes 110600 | tf_op jit(solution)/shard_map/ppermute | solution.py:289
  27.2 1.5 %collective-permute-start.13 = (bf16[32,2048]{1,0:T(8,128)(2,1)S(1)}, bf16[32,2048]{1,0:T(8,128)(2,1)S(1)}, u32[]{:S(2)}, u32[]{:S(2)}) collective-permute-start(bf16[32,2048]{1,0:T(8,128)(2,1)S(1)} %get-tuple-element.82.refs_0_), channel_id=1, source_target_pairs={{0,24},{1,25},{2,26},{3,27},{4,28},{5,29},{6,30},{7,31},{8,16},{9,... | collective-permute-start | bytes 393224 | tf_op jit(solution)/shard_map/ppermute | solution.py:463
  28.6 0.0 collective-permute-start.12
  28.6 2.9 %collective-permute-start.11 = (bf16[32,2048]{1,0:T(8,128)(2,1)S(1)}, bf16[32,2048]{1,0:T(8,128)(2,1)S(1)}, u32[]{:S(2)}, u32[]{:S(2)}) collective-permute-start(bf16[32,2048]{1,0:T(8,128)(2,1)S(1)} %get-tuple-element.82.refs_0_), channel_id=1, source_target_pairs={{0,8},{1,9},{2,10},{3,11},{4,12},{5,13},{6,14},{7,15},{8,0},{9,1},... | collective-permute-start | bytes 393224 | tf_op jit(solution)/shard_map/ppermute | solution.py:463
  31.5 0.0 collective-permute-done.6.other_ref
  31.5 0.7 collective-permute-done.5.received_ref
  32.3 0.1 join_plane.2.refs_0_
  32.4 1.6 %collective-permute-start.10 = (bf16[256,2176]{1,0:T(8,128)(2,1)S(1)}, bf16[256,2176]{1,0:T(8,128)(2,1)S(1)}, u32[]{:S(2)}, u32[]{:S(2)}) collective-permute-start(bf16[256,2176]{1,0:T(8,128)(2,1)S(1)} %join_plane.2.refs_0_), channel_id=1, source_target_pairs={{0,2},{1,3},{2,0},{3,1},{4,5},{5,4},{6,7},{7,6},{8,10},{9,11},{10,... | collective-permute-start | bytes 3342344 | tf_op jit(solution)/shard_map/ppermute | solution.py:763
  33.9 8.5 %adjoint_scan.1 = (bf16[128,1024]{1,0:T(8,128)(2,1)}, bf16[128,1024]{1,0:T(8,128)(2,1)}, f32[2,16,128]{2,1,0:T(8,128)S(1)}, f32[16,1024]{1,0:T(8,128)S(1)}, bf16[3,896,2048]{2,1,0:T(8,128)(2,1)S(1)}) custom-call(f32[128,1024]{1,0:T(8,128)S(1)} %get-tuple-element.55.step_v, f32[128,1024]{1,0:T(8,128)S(1)} %get-tuple-element.56.drive_v, ...), custom_call_target="tpu_custom_call" | custom-call | flops 13799999488 | tf_op jit(solution)/shard_map/adjoint_scan/pallas_call | solution.py:354
  42.4 0.0 copy-start
  42.5 0.1 collective-permute-start.8
  42.5 1.2 %collective-permute-done.8.two_ref = f32[16,1024]{1,0:T(8,128)S(1)} collective-permute-done((f32[16,1024]{1,0:T(8,128)S(1)}, f32[16,1024]{1,0:T(8,128)S(1)}, u32[]{:S(2)}, u32[]{:S(2)}) %collective-permute-start.8) | collective-permute-done | bytes 65568 | tf_op jit(solution)/shard_map/ppermute | solution.py:779
  43.8 1.5 %collective-permute-start.7 = (f32[2,16,128]{2,1,0:T(8,128)S(1)}, f32[2,16,128]{2,1,0:T(8,128)S(1)}, u32[]{:S(2)}, u32[]{:S(2)}) collective-permute-start(f32[2,16,128]{2,1,0:T(8,128)S(1)} %get-tuple-element.78.one_ref), channel_id=1, source_target_pairs={{0,1},{1,0},{2,3},{3,2},{4,5},{5,4},{6,7},{7,6},{8,9},{9,8},{10,11... | collective-permute-start | bytes 49160 | tf_op jit(solution)/shard_map/ppermute | solution.py:780
  45.3 2.2 %collective-permute-done.7.two_ref = f32[2,16,128]{2,1,0:T(8,128)S(1)} collective-permute-done((f32[2,16,128]{2,1,0:T(8,128)S(1)}, f32[2,16,128]{2,1,0:T(8,128)S(1)}, u32[]{:S(2)}, u32[]{:S(2)}) %collective-permute-start.7) | collective-permute-done | bytes 16416 | tf_op jit(solution)/shard_map/ppermute | solution.py:780
  47.5 0.0 collective-permute-done.13.refs_3_
  47.5 0.0 collective-permute-done.12.refs_2_
  47.5 0.0 collective-permute-done.11.refs_1_
  47.6 1.6 %collective-permute-start.18 = (bf16[4,32,2048]{2,1,0:T(8,128)(2,1)S(1)}, bf16[4,32,2048]{2,1,0:T(8,128)(2,1)S(1)}, u32[]{:S(2)}, u32[]{:S(2)}) collective-permute-start(bf16[4,32,2048]{2,1,0:T(8,128)(2,1)S(1)} %join_z.3.held_ref), channel_id=1, source_target_pairs={{0,1},{1,0},{2,3},{3,2},{4,6},{5,7},{6,4},{7,5},{8,9},{9,8},{10,11... | collective-permute-start | bytes 1572872 | tf_op jit(solution)/shard_map/ppermute | solution.py:785
  49.2 2.0 %collective-permute-start.14 = (bf16[16,1024]{1,0:T(8,128)(2,1)S(1)}, bf16[16,1024]{1,0:T(8,128)(2,1)S(1)}, u32[]{:S(2)}, u32[]{:S(2)}) collective-permute-start(bf16[16,1024]{1,0:T(8,128)(2,1)S(1)} %add_two.4.one_ref), channel_id=1, source_target_pairs={{0,8},{1,9},{2,10},{3,11},{4,12},{5,13},{6,14},{7,15},{8,0},{9,1},... | collective-permute-start | bytes 98312 | tf_op jit(solution)/shard_map/ppermute | solution.py:786
  51.2 1.9 %collective-permute-done.14.two_ref = bf16[16,1024]{1,0:T(8,128)(2,1)S(1)} collective-permute-done((bf16[16,1024]{1,0:T(8,128)(2,1)S(1)}, bf16[16,1024]{1,0:T(8,128)(2,1)S(1)}, u32[]{:S(2)}, u32[]{:S(2)}) %collective-permute-start.14) | collective-permute-done | bytes 32800 | tf_op jit(solution)/shard_map/ppermute | solution.py:786
  53.1 0.0 collective-permute-done.10.refs_1_
  53.1 0.1 collective-permute-start.16
  53.2 0.5 collective-permute-start.15
  53.7 3.2 %collective-permute-done.18.received_ref = bf16[4,32,2048]{2,1,0:T(8,128)(2,1)S(1)} collective-permute-done((bf16[4,32,2048]{2,1,0:T(8,128)(2,1)S(1)}, bf16[4,32,2048]{2,1,0:T(8,128)(2,1)S(1)}, u32[]{:S(2)}, u32[]{:S(2)}) %collective-permute-start.18) | collective-permute-done | bytes 524320 | tf_op jit(solution)/shard_map/ppermute | solution.py:785
  56.8 0.1 join_plane.3.refs_0_
  56.9 0.6 collective-permute-start.19
  57.5 2.9 %collective-permute-start.17 = (bf16[16,1024]{1,0:T(8,128)(2,1)S(1)}, bf16[16,1024]{1,0:T(8,128)(2,1)S(1)}, u32[]{:S(2)}, u32[]{:S(2)}) collective-permute-start(bf16[16,1024]{1,0:T(8,128)(2,1)S(1)} %add_two.6.one_ref), channel_id=1, source_target_pairs={{0,16},{1,17},{2,18},{3,19},{4,20},{5,21},{6,22},{7,23},{8,24},{9,... | collective-permute-start | bytes 98312 | tf_op jit(solution)/shard_map/ppermute | solution.py:788
  60.4 1.5 %collective-permute-start.9 = (f32[2,16,128]{2,1,0:T(8,128)S(1)}, f32[2,16,128]{2,1,0:T(8,128)S(1)}, u32[]{:S(2)}, u32[]{:S(2)}) collective-permute-start(f32[2,16,128]{2,1,0:T(8,128)S(1)} %add_two.5.one_ref), channel_id=1, source_target_pairs={{0,2},{1,3},{2,0},{3,1},{4,6},{5,7},{6,4},{7,5},{8,10},{9,11},{10,... | collective-permute-start | bytes 49160 | tf_op jit(solution)/shard_map/ppermute | solution.py:783
  61.9 0.4 collective-permute-done.17.two_ref
  62.3 0.0 collective-permute-start.20
  62.3 0.6 add_two.7
  63.0 0.0 collective-permute-done.16.refs_3_
  63.0 0.0 collective-permute-done.15.refs_2_
  63.0 0.0 copy-done
  63.0 11.2 %experts_0.1 = (bf16[4,896,4096]{2,1,0:T(8,128)(2,1)}, f32[4,256,896]{2,1,0:T(8,128)S(1)}, bf16[4,256,256]{2,1,0:T(8,128)(2,1)S(1)}, f32[4,256,128]{2,1,0:T(8,128)S(1)}) custom-call(bf16[256,2176]{1,0:T(8,128)(2,1)S(1)} %join_plane.2.refs_0_, bf16[256,2176]{1,0:T(8,128)(2,1)S(1)} %collective-permute-done.10.refs_1_, ...), custom_call_target="tpu_custom_call" | custom-call | tf_op jit(solution)/shard_map/experts_0/pallas_call | solution.py:683
  74.2 0.0 collective-permute-done.9.two_ref
  74.2 0.6 split_add.1
  74.8 0.0 collective-permute-done.19.refs_1_
  74.8 0.5 collective-permute-start.21
  75.3 0.0 collective-permute-done.20.refs_2_
  75.3 2.3 %collective-permute-done.21.refs_3_ = bf16[256,2048]{1,0:T(8,128)(2,1)S(1)} collective-permute-done((bf16[256,2048]{1,0:T(8,128)(2,1)S(1)}, bf16[256,2048]{1,0:T(8,128)(2,1)S(1)}, u32[]{:S(2)}, u32[]{:S(2)}) %collective-permute-start.21) | collective-permute-done | bytes 1048608 | tf_op jit(solution)/shard_map/ppermute | solution.py:801
  77.6 12.0 %experts_1.1 = (bf16[4,896,4096]{2,1,0:T(8,128)(2,1)}, bf16[4,256,896]{2,1,0:T(8,128)(2,1)}) custom-call(bf16[256,2048]{1,0:T(8,128)(2,1)S(1)} %join_plane.3.refs_0_, bf16[256,2048]{1,0:T(8,128)(2,1)S(1)} %collective-permute-done.19.refs_1_, bf16[256,2048]{1,0:T(8,128)(2,1)S(1)} %collective-permute-done.20.refs_2_, ...), custom_call_target="tpu_custom_call", output_to_operand_aliasing={{0}: (10, {})} | custom-call | tf_op jit(solution)/shard_map/experts_1/pallas_call | solution.py:683
  (5 shorter events, 0.1 us)
Async XLA Ops:
  5.5 17.1 %collective-permute-start.4 = (bf16[32,2176]{1,0:T(8,128)(2,1)S(1)}, bf16[32,2176]{1,0:T(8,128)(2,1)S(1)}, u32[]{:S(2)}, u32[]{:S(2)}) collective-permute-start(bf16[32,2176]{1,0:T(8,128)(2,1)S(1)} %get-tuple-element.62.refs_0_), channel_id=1, source_target_pairs={{0,24},{1,25},{2,26},{3,27},{4,28},{5,29},{6,30},{7,31},{8,16},{9,... | collective-permute-start | bytes 417800 | tf_op jit(solution)/shard_map/ppermute | solution.py:463
  10.6 12.0 %collective-permute-start.3 = (bf16[32,2176]{1,0:T(8,128)(2,1)S(1)}, bf16[32,2176]{1,0:T(8,128)(2,1)S(1)}, u32[]{:S(2)}, u32[]{:S(2)}) collective-permute-start(bf16[32,2176]{1,0:T(8,128)(2,1)S(1)} %get-tuple-element.62.refs_0_), channel_id=1, source_target_pairs={{0,16},{1,17},{2,18},{3,19},{4,20},{5,21},{6,22},{7,23},{8,24},{9,... | collective-permute-start | bytes 417800 | tf_op jit(solution)/shard_map/ppermute | solution.py:463
  10.6 12.0 %collective-permute-start.2 = (bf16[32,2176]{1,0:T(8,128)(2,1)S(1)}, bf16[32,2176]{1,0:T(8,128)(2,1)S(1)}, u32[]{:S(2)}, u32[]{:S(2)}) collective-permute-start(bf16[32,2176]{1,0:T(8,128)(2,1)S(1)} %get-tuple-element.62.refs_0_), channel_id=1, source_target_pairs={{0,8},{1,9},{2,10},{3,11},{4,12},{5,13},{6,14},{7,15},{8,0},{9,1},... | collective-permute-start | bytes 417800 | tf_op jit(solution)/shard_map/ppermute | solution.py:463
  11.2 1.3 %collective-permute-start = (f32[17,1024]{1,0:T(8,128)S(1)}, f32[17,1024]{1,0:T(8,128)S(1)}, u32[]{:S(2)}, u32[]{:S(2)}) collective-permute-start(f32[17,1024]{1,0:T(8,128)S(1)} %get-tuple-element.59.total_ref), channel_id=1, source_target_pairs={{0,4},{4,0},{8,12},{12,8},{16,20},{20,16},{24,28},{28,24},{1,5},{5... | collective-permute-start | bytes 208904 | tf_op jit(solution)/shard_map/ppermute | solution.py:289
  13.4 7.7 %collective-permute-start.1 = (bf16[18,1024]{1,0:T(8,128)(2,1)S(1)}, bf16[18,1024]{1,0:T(8,128)(2,1)S(1)}, u32[]{:S(2)}, u32[]{:S(2)}) collective-permute-start(bf16[18,1024]{1,0:T(8,128)(2,1)S(1)} %get-tuple-element.66), channel_id=1, source_target_pairs={{0,8},{4,12},{8,0},{12,4},{16,24},{20,28},{24,16},{28,20},{1,9},{5... | collective-permute-start | bytes 110600 | tf_op jit(solution)/shard_map/ppermute | solution.py:289
  22.7 9.6 %collective-permute-start.5 = (bf16[4,32,2176]{2,1,0:T(8,128)(2,1)S(1)}, bf16[4,32,2176]{2,1,0:T(8,128)(2,1)S(1)}, u32[]{:S(2)}, u32[]{:S(2)}) collective-permute-start(bf16[4,32,2176]{2,1,0:T(8,128)(2,1)S(1)} %join_z.2.held_ref), channel_id=1, source_target_pairs={{0,1},{1,0},{2,3},{3,2},{4,6},{5,7},{6,4},{7,5},{8,9},{9,8},{10,11... | collective-permute-start | bytes 1671176 | tf_op jit(solution)/shard_map/ppermute | solution.py:759
  24.2 7.3 %collective-permute-start.6 = (bf16[18,1024]{1,0:T(8,128)(2,1)S(1)}, bf16[18,1024]{1,0:T(8,128)(2,1)S(1)}, u32[]{:S(2)}, u32[]{:S(2)}) collective-permute-start(bf16[18,1024]{1,0:T(8,128)(2,1)S(1)} %get-tuple-element.73), channel_id=1, source_target_pairs={{0,16},{4,20},{8,24},{12,28},{16,0},{20,4},{24,8},{28,12},{1,17},{... | collective-permute-start | bytes 110600 | tf_op jit(solution)/shard_map/ppermute | solution.py:289
  27.2 20.4 %collective-permute-start.13 = (bf16[32,2048]{1,0:T(8,128)(2,1)S(1)}, bf16[32,2048]{1,0:T(8,128)(2,1)S(1)}, u32[]{:S(2)}, u32[]{:S(2)}) collective-permute-start(bf16[32,2048]{1,0:T(8,128)(2,1)S(1)} %get-tuple-element.82.refs_0_), channel_id=1, source_target_pairs={{0,24},{1,25},{2,26},{3,27},{4,28},{5,29},{6,30},{7,31},{8,16},{9,... | collective-permute-start | bytes 393224 | tf_op jit(solution)/shard_map/ppermute | solution.py:463
  28.6 18.9 %collective-permute-start.12 = (bf16[32,2048]{1,0:T(8,128)(2,1)S(1)}, bf16[32,2048]{1,0:T(8,128)(2,1)S(1)}, u32[]{:S(2)}, u32[]{:S(2)}) collective-permute-start(bf16[32,2048]{1,0:T(8,128)(2,1)S(1)} %get-tuple-element.82.refs_0_), channel_id=1, source_target_pairs={{0,16},{1,17},{2,18},{3,19},{4,20},{5,21},{6,22},{7,23},{8,24},{9,... | collective-permute-start | bytes 393224 | tf_op jit(solution)/shard_map/ppermute | solution.py:463
  28.6 18.9 %collective-permute-start.11 = (bf16[32,2048]{1,0:T(8,128)(2,1)S(1)}, bf16[32,2048]{1,0:T(8,128)(2,1)S(1)}, u32[]{:S(2)}, u32[]{:S(2)}) collective-permute-start(bf16[32,2048]{1,0:T(8,128)(2,1)S(1)} %get-tuple-element.82.refs_0_), channel_id=1, source_target_pairs={{0,8},{1,9},{2,10},{3,11},{4,12},{5,13},{6,14},{7,15},{8,0},{9,1},... | collective-permute-start | bytes 393224 | tf_op jit(solution)/shard_map/ppermute | solution.py:463
  32.4 20.7 %collective-permute-start.10 = (bf16[256,2176]{1,0:T(8,128)(2,1)S(1)}, bf16[256,2176]{1,0:T(8,128)(2,1)S(1)}, u32[]{:S(2)}, u32[]{:S(2)}) collective-permute-start(bf16[256,2176]{1,0:T(8,128)(2,1)S(1)} %join_plane.2.refs_0_), channel_id=1, source_target_pairs={{0,2},{1,3},{2,0},{3,1},{4,5},{5,4},{6,7},{7,6},{8,10},{9,11},{10,... | collective-permute-start | bytes 3342344 | tf_op jit(solution)/shard_map/ppermute | solution.py:763
  42.4 20.5 %copy-start = (bf16[4,256,896]{2,1,0:T(8,128)(2,1)S(1)}, bf16[4,256,896]{2,1,0:T(8,128)(2,1)}, u32[]{:S(2)}) copy-start(bf16[4,256,896]{2,1,0:T(8,128)(2,1)} %refs_4_.3) | copy-start | bytes 5505028
  42.5 1.3 %collective-permute-start.8 = (f32[16,1024]{1,0:T(8,128)S(1)}, f32[16,1024]{1,0:T(8,128)S(1)}, u32[]{:S(2)}, u32[]{:S(2)}) collective-permute-start(f32[16,1024]{1,0:T(8,128)S(1)} %get-tuple-element.79.one_ref), channel_id=1, source_target_pairs={{0,4},{1,5},{2,6},{3,7},{4,0},{5,1},{6,2},{7,3},{8,12},{9,13},{10,... | collective-permute-start | bytes 196616 | tf_op jit(solution)/shard_map/ppermute | solution.py:779
  43.8 3.7 %collective-permute-start.7 = (f32[2,16,128]{2,1,0:T(8,128)S(1)}, f32[2,16,128]{2,1,0:T(8,128)S(1)}, u32[]{:S(2)}, u32[]{:S(2)}) collective-permute-start(f32[2,16,128]{2,1,0:T(8,128)S(1)} %get-tuple-element.78.one_ref), channel_id=1, source_target_pairs={{0,1},{1,0},{2,3},{3,2},{4,5},{5,4},{6,7},{7,6},{8,9},{9,8},{10,11... | collective-permute-start | bytes 49160 | tf_op jit(solution)/shard_map/ppermute | solution.py:780
  47.6 9.2 %collective-permute-start.18 = (bf16[4,32,2048]{2,1,0:T(8,128)(2,1)S(1)}, bf16[4,32,2048]{2,1,0:T(8,128)(2,1)S(1)}, u32[]{:S(2)}, u32[]{:S(2)}) collective-permute-start(bf16[4,32,2048]{2,1,0:T(8,128)(2,1)S(1)} %join_z.3.held_ref), channel_id=1, source_target_pairs={{0,1},{1,0},{2,3},{3,2},{4,6},{5,7},{6,4},{7,5},{8,9},{9,8},{10,11... | collective-permute-start | bytes 1572872 | tf_op jit(solution)/shard_map/ppermute | solution.py:785
  49.2 3.9 %collective-permute-start.14 = (bf16[16,1024]{1,0:T(8,128)(2,1)S(1)}, bf16[16,1024]{1,0:T(8,128)(2,1)S(1)}, u32[]{:S(2)}, u32[]{:S(2)}) collective-permute-start(bf16[16,1024]{1,0:T(8,128)(2,1)S(1)} %add_two.4.one_ref), channel_id=1, source_target_pairs={{0,8},{1,9},{2,10},{3,11},{4,12},{5,13},{6,14},{7,15},{8,0},{9,1},... | collective-permute-start | bytes 98312 | tf_op jit(solution)/shard_map/ppermute | solution.py:786
  53.1 9.9 %collective-permute-start.16 = (bf16[256,2176]{1,0:T(8,128)(2,1)S(1)}, bf16[256,2176]{1,0:T(8,128)(2,1)S(1)}, u32[]{:S(2)}, u32[]{:S(2)}) collective-permute-start(bf16[256,2176]{1,0:T(8,128)(2,1)S(1)} %collective-permute-done.10.refs_1_), channel_id=1, source_target_pairs={{0,4},{1,5},{2,6},{3,7},{4,0},{5,1},{6,2},{7,3},{8,12},{9,13},{10,... | collective-permute-start | bytes 3342344 | tf_op jit(solution)/shard_map/ppermute | solution.py:790
  53.2 9.8 %collective-permute-start.15 = (bf16[256,2176]{1,0:T(8,128)(2,1)S(1)}, bf16[256,2176]{1,0:T(8,128)(2,1)S(1)}, u32[]{:S(2)}, u32[]{:S(2)}) collective-permute-start(bf16[256,2176]{1,0:T(8,128)(2,1)S(1)} %join_plane.2.refs_0_), channel_id=1, source_target_pairs={{0,4},{1,5},{2,6},{3,7},{4,0},{5,1},{6,2},{7,3},{8,12},{9,13},{10,... | collective-permute-start | bytes 3342344 | tf_op jit(solution)/shard_map/ppermute | solution.py:764
  56.9 17.9 %collective-permute-start.19 = (bf16[256,2048]{1,0:T(8,128)(2,1)S(1)}, bf16[256,2048]{1,0:T(8,128)(2,1)S(1)}, u32[]{:S(2)}, u32[]{:S(2)}) collective-permute-start(bf16[256,2048]{1,0:T(8,128)(2,1)S(1)} %join_plane.3.refs_0_), channel_id=1, source_target_pairs={{0,2},{1,3},{2,0},{3,1},{4,5},{5,4},{6,7},{7,6},{8,10},{9,11},{10,... | collective-permute-start | bytes 3145736 | tf_op jit(solution)/shard_map/ppermute | solution.py:793
  57.5 4.8 %collective-permute-start.17 = (bf16[16,1024]{1,0:T(8,128)(2,1)S(1)}, bf16[16,1024]{1,0:T(8,128)(2,1)S(1)}, u32[]{:S(2)}, u32[]{:S(2)}) collective-permute-start(bf16[16,1024]{1,0:T(8,128)(2,1)S(1)} %add_two.6.one_ref), channel_id=1, source_target_pairs={{0,16},{1,17},{2,18},{3,19},{4,20},{5,21},{6,22},{7,23},{8,24},{9,... | collective-permute-start | bytes 98312 | tf_op jit(solution)/shard_map/ppermute | solution.py:788
  60.4 13.8 %collective-permute-start.9 = (f32[2,16,128]{2,1,0:T(8,128)S(1)}, f32[2,16,128]{2,1,0:T(8,128)S(1)}, u32[]{:S(2)}, u32[]{:S(2)}) collective-permute-start(f32[2,16,128]{2,1,0:T(8,128)S(1)} %add_two.5.one_ref), channel_id=1, source_target_pairs={{0,2},{1,3},{2,0},{3,1},{4,6},{5,7},{6,4},{7,5},{8,10},{9,11},{10,... | collective-permute-start | bytes 49160 | tf_op jit(solution)/shard_map/ppermute | solution.py:783
  62.3 13.0 %collective-permute-start.20 = (bf16[256,2048]{1,0:T(8,128)(2,1)S(1)}, bf16[256,2048]{1,0:T(8,128)(2,1)S(1)}, u32[]{:S(2)}, u32[]{:S(2)}) collective-permute-start(bf16[256,2048]{1,0:T(8,128)(2,1)S(1)} %join_plane.3.refs_0_), channel_id=1, source_target_pairs={{0,4},{1,5},{2,6},{3,7},{4,0},{5,1},{6,2},{7,3},{8,12},{9,13},{10,... | collective-permute-start | bytes 3145736 | tf_op jit(solution)/shard_map/ppermute | solution.py:794
  74.8 2.8 %collective-permute-start.21 = (bf16[256,2048]{1,0:T(8,128)(2,1)S(1)}, bf16[256,2048]{1,0:T(8,128)(2,1)S(1)}, u32[]{:S(2)}, u32[]{:S(2)}) collective-permute-start(bf16[256,2048]{1,0:T(8,128)(2,1)S(1)} %collective-permute-done.19.refs_1_), channel_id=1, source_target_pairs={{0,4},{1,5},{2,6},{3,7},{4,0},{5,1},{6,2},{7,3},{8,12},{9,13},{10,... | collective-permute-start | bytes 3145736 | tf_op jit(solution)/shard_map/ppermute | solution.py:801
